TPU v7x, 512 devices: a whole 4x4x16 slice. The times are simulated.
512 devices in a mesh: scen: 4 (over x), gx: 8 (over y, core), gy: 16 (over z).
Axes of the slice: x: 4, y: 4, z: 16, core: 2. Of those that a mesh axis runs over, the one named last changes fastest.
Arguments:
- perm_log: float32 [2, 512, 2048], P(None, 'gx', 'gy'), may hold values from -2.5 to 2.5
- facies: int32 [2, 512, 2048], P(None, 'gx', 'gy'), may hold values from 0 to 3
- facies_scale: float32 [4], replicated, may hold values from 0.5 to 2
- accumulation: float32 [2, 512, 2048], P(None, 'gx', 'gy'), may hold values from 0.05 to 0.5
- previous_pressure: float32 [4, 2, 512, 2048], P('scen', None, 'gx', 'gy'), may hold values from -6 to 6
- observed: float32 [4, 2, 512, 2048], P('scen', None, 'gx', 'gy'), may hold values from -6 to 6
- well_cells: int32 [4, 5], P('scen'), may hold values from 0 to 2097151
- well_rates: float32 [4, 5], P('scen'), may hold values from 5 to 20
Outputs:
- pressure: float32 [4, 2, 512, 2048], P('scen', None, 'gx', 'gy')
- adjoint: float32 [4, 2, 512, 2048], P('scen', None, 'gx', 'gy')
- gradient: float32 [2, 512, 2048], P(None, 'gx', 'gy')
Inputs may be any that keep to these rules, and one draw needn't show every extreme that they name: `well_cells`: a flat index layer * 512 * 2048 + row * 2048 + column of a grid cell; several wells may share a cell.
All inputs are finite; a program needn't handle non-finite values.
Results may differ from a plain program's by a relative error of at most 0.0001.
Values sent between devices are 32-bit elements; how exact they have to be, the bound alone decides.
A program may use at most 128 MiB of HBM per device.

v0:
```python
from functools import partial

import jax
import jax.numpy as jnp
from jax import lax
from jax.sharding import PartitionSpec as P

WELLS = 5
FACIES = 4
SMOOTH = 2
COARSE = 4


vertical = 0.3
damping = 0.8


def extended(block, sides, width):
    for axis, dim in sides:
        count = lax.axis_size(axis)
        forward = [(i, i + 1) for i in range(count - 1)]
        backward = [(target, source) for source, target in forward]
        low = lax.ppermute(
            lax.slice_in_dim(block, block.shape[dim] - width, None, axis=dim), axis, forward
        )
        high = lax.ppermute(lax.slice_in_dim(block, 0, width, axis=dim), axis, backward)
        block = jnp.concatenate([low, block, high], axis=dim)
    return block


def passed_along(value, axis, steps):
    count = lax.axis_size(axis)
    first, last = (max(0, -steps), min(count, count - steps))
    return lax.ppermute(value, axis, [(source, source + steps) for source in range(first, last)])


def partner(value, axis, distance):
    return lax.ppermute(value, axis, [(i, i ^ 1 << distance) for i in range(lax.axis_size(axis))])


def harmonic(left, right):
    return 2.0 * left * right / (left + right)


def planar(padded):
    return (
        padded[..., :-2, 1:-1],
        padded[..., 2:, 1:-1],
        padded[..., 1:-1, :-2],
        padded[..., 1:-1, 2:],
    )


def layer_pair(values):
    padded = jnp.pad(values, ((1, 1), (0, 0), (0, 0)))
    return (padded[:-2], padded[2:])


def build_coeffs(permeability, beside, accumulation):
    below, above = layer_pair(permeability)
    return jnp.stack(
        [
            harmonic(permeability, beside[0]),
            harmonic(permeability, beside[1]),
            harmonic(permeability, beside[2]),
            harmonic(permeability, beside[3]),
            vertical * harmonic(permeability, below),
            vertical * harmonic(permeability, above),
            accumulation,
        ]
    )


def coarsen(coeffs):
    member_count, layer_count, row_count, col_count = coeffs.shape
    quads = coeffs.reshape(member_count, layer_count, row_count // 2, 2, col_count // 2, 2)
    return jnp.stack(
        [
            quads[0, :, :, 0, :, 0] + quads[0, :, :, 0, :, 1],
            quads[1, :, :, 1, :, 0] + quads[1, :, :, 1, :, 1],
            quads[2, :, :, 0, :, 0] + quads[2, :, :, 1, :, 0],
            quads[3, :, :, 0, :, 1] + quads[3, :, :, 1, :, 1],
            jnp.sum(quads[4], (2, 4)),
            jnp.sum(quads[5], (2, 4)),
            jnp.sum(quads[6], (2, 4)),
        ]
    )


def restrict(values):
    layer_count, row_count, col_count = values.shape
    return values.reshape(layer_count, row_count // 2, 2, col_count // 2, 2).sum((2, 4))


def upsample(values):
    return jnp.repeat(jnp.repeat(values, 2, 1), 2, 2)


def parity(bit_number):
    return lax.axis_index("gy") // 2**bit_number % 2


def join_halves(own_half, other_half, bit_number, axis_number):
    lower = parity(bit_number) == 0
    first = jnp.where(lower, own_half, other_half)
    second = jnp.where(lower, other_half, own_half)
    return jnp.concatenate([first, second], axis_number)


def take_half(values, bit_number):
    half_width = values.shape[2] // 2
    return lax.dynamic_slice_in_dim(values, parity(bit_number) * half_width, half_width, 2)


def fine_neighbours(values):
    return planar(extended(values, (("gx", 1), ("gy", 2)), 1))


def coarse_neighbours(values, distance):
    row_lo = passed_along(values[:, -1:, :], "gx", 1)
    row_hi = passed_along(values[:, :1, :], "gx", -1)
    col_lo = passed_along(values[:, :, -1:], "gy", distance)
    col_hi = passed_along(values[:, :, :1], "gy", -distance)
    return (
        jnp.concatenate([row_lo, values[:, :-1, :]], 1),
        jnp.concatenate([values[:, 1:, :], row_hi], 1),
        jnp.concatenate([col_lo, values[:, :, :-1]], 2),
        jnp.concatenate([values[:, :, 1:], col_hi], 2),
    )


def apply_op(values, grid_level, neighbours):
    coeffs, diagonal = grid_level
    row_lo, row_hi, col_lo, col_hi = neighbours(values)
    layer_lo, layer_hi = layer_pair(values)
    return diagonal * values - (
        coeffs[0] * row_lo
        + coeffs[1] * row_hi
        + coeffs[2] * col_lo
        + coeffs[3] * col_hi
        + coeffs[4] * layer_lo
        + coeffs[5] * layer_hi
    )


def smooth(values, target, grid_level, neighbours, sweeps):
    for _ in range(sweeps):
        values = (
            values + damping * (target - apply_op(values, grid_level, neighbours)) / grid_level[1]
        )
    return values


def lift_middle(values):
    return join_halves(values, partner(values, "gy", 0), 0, 2)


def lift_bottom(values):
    return join_halves(values, partner(values, "gy", 1), 1, 2)


def drop_bottom(values):
    return take_half(values, 1)


def drop_middle(values):
    return take_half(values, 0)


def vcycle(target, initial, grids):
    finest, middle, bottom = grids
    middle_near = partial(coarse_neighbours, distance=2)
    bottom_near = partial(coarse_neighbours, distance=4)
    fine_field = smooth(initial, target, finest, fine_neighbours, SMOOTH)
    middle_target = lift_middle(restrict(target - apply_op(fine_field, finest, fine_neighbours)))
    middle_field = smooth(jnp.zeros_like(middle_target), middle_target, middle, middle_near, SMOOTH)
    bottom_target = lift_bottom(
        restrict(middle_target - apply_op(middle_field, middle, middle_near))
    )
    bottom_field = smooth(jnp.zeros_like(bottom_target), bottom_target, bottom, bottom_near, COARSE)
    middle_field = smooth(
        middle_field + upsample(drop_bottom(bottom_field)),
        middle_target,
        middle,
        middle_near,
        SMOOTH,
    )
    fine_field = fine_field + upsample(drop_middle(middle_field))
    return smooth(fine_field, target, finest, fine_neighbours, SMOOTH)


def face_term(permeability, perm_side, pressure, pressure_side, adjoint, adjoint_side, weight):
    total_perm = permeability + perm_side
    return (
        weight
        * permeability
        * 2.0
        * perm_side
        * perm_side
        / (total_perm * total_perm)
        * (adjoint - adjoint_side)
        * (pressure - pressure_side)
    )


def gradient_terms(permeability, perm_six, pressure, pressure_six, adjoint, adjoint_six):
    weights = (1.0, 1.0, 1.0, 1.0, vertical, vertical)
    total = jnp.zeros_like(permeability)
    for number in range(6):
        total = total + face_term(
            permeability,
            perm_six[number],
            pressure,
            pressure_six[number],
            adjoint,
            adjoint_six[number],
            weights[number],
        )
    return total


def with_diagonal(coeffs):
    return (coeffs, jnp.sum(coeffs, 0))


def shards(
    perm_log,
    facies,
    facies_scale,
    accumulation,
    previous_pressure,
    observed,
    well_cells,
    well_rates,
):
    facies_factor = jnp.zeros_like(perm_log)
    for label in range(FACIES):
        facies_factor = facies_factor + jnp.where(
            facies == label, facies_scale[label], jnp.float32(0.0)
        )
    permeability = jnp.exp(perm_log) * facies_factor
    perm_padded = extended(permeability, (("gx", 1), ("gy", 2)), 1)
    perm_beside = planar(perm_padded)
    coeffs = build_coeffs(permeability, perm_beside, accumulation)
    middle = coarsen(coeffs)
    middle = join_halves(middle, partner(middle, "gy", 0), 0, 3)
    bottom = coarsen(middle)
    bottom = join_halves(bottom, partner(bottom, "gy", 1), 1, 3)
    grids = (with_diagonal(coeffs), with_diagonal(middle), with_diagonal(bottom))
    layer_count, row_count, col_count = perm_log.shape
    total_rows = row_count * lax.axis_size("gx")
    total_cols = col_count * lax.axis_size("gy")
    plane_size = total_rows * total_cols
    well_index = well_cells[0]
    well_rate = well_rates[0]
    layer_of = well_index // plane_size
    remainder = well_index % plane_size
    row_of = remainder // total_cols - lax.axis_index("gx") * row_count
    col_of = remainder % total_cols - lax.axis_index("gy") * col_count
    layer_iota = lax.broadcasted_iota(jnp.int32, perm_log.shape, 0)
    row_iota = lax.broadcasted_iota(jnp.int32, perm_log.shape, 1)
    col_iota = lax.broadcasted_iota(jnp.int32, perm_log.shape, 2)
    source = jnp.zeros_like(perm_log)
    for number in range(WELLS):
        placed = (
            (layer_iota == layer_of[number])
            & (row_iota == row_of[number])
            & (col_iota == col_of[number])
        )
        source = source + jnp.where(placed, well_rate[number], jnp.float32(0.0))
    start_pressure = previous_pressure[0]
    pressure = vcycle(accumulation * start_pressure + source, start_pressure, grids)
    adjoint = vcycle(pressure - observed[0], jnp.zeros_like(pressure), grids)
    states = extended(jnp.stack([pressure, adjoint]), (("gx", 2), ("gy", 3)), 1)
    state_beside = planar(states)
    pressure_six = tuple((shifted[0] for shifted in state_beside)) + layer_pair(pressure)
    adjoint_six = tuple((shifted[1] for shifted in state_beside)) + layer_pair(adjoint)
    perm_six = perm_beside + layer_pair(permeability)
    local_terms = gradient_terms(
        permeability, perm_six, pressure, pressure_six, adjoint, adjoint_six
    )
    gradient = lax.psum(-local_terms, "scen")
    return (pressure[None], adjoint[None], gradient)


def solution(mesh):
    return jax.shard_map(
        shards,
        mesh=mesh,
        in_specs=(
            P(None, "gx", "gy"),
            P(None, "gx", "gy"),
            P(),
            P(None, "gx", "gy"),
            P("scen", None, "gx", "gy"),
            P("scen", None, "gx", "gy"),
            P("scen", None),
            P("scen", None),
        ),
        out_specs=(P("scen", None, "gx", "gy"), P("scen", None, "gx", "gy"), P(None, "gx", "gy")),
        check_vma=False,
    )
```

profile of v0, /device:TPU:1, one launch (start us, length us, event | category | flops | bytes accessed | tf_op | source)
XLA Modules:
  0.0 733.3 jit_solution(14104127745226850391)
XLA Ops:
  12.1 4.6 collective-permute-start
  16.7 5.5 collective-permute-start.1
  49.0 4.2 collective-permute-start.6
  54.5 6.3 squeeze.134
  65.6 6.7 collective-permute-start.20
  82.4 5.5 stack.54
  87.9 4.5 fusion.414
  95.4 5.5 stack.26
  104.5 5.5 stack.55
  117.1 5.5 stack.56
  122.6 4.8 fusion.412
  130.5 4.6 collective-permute-start.10
  136.5 5.5 squeeze.132
  155.1 5.5 squeeze.133
  163.6 5.2 collective-permute-start.14
  177.6 5.5 reshape.243
  194.2 5.8 collective-permute-done.17
  200.6 9.4 %collective-permute-start.32 = (f32[2,16,1]{2,1,0:T(8,128)}, f32[2,16,1]{2,1,0:T(8,128)}, u32[]{:S(2)}, u32[]{:S(2)}) collective-permute-start(f32[2,16,1]{2,1,0:T(8,128)} %broadcast.184), channel_id=1, source_target_pairs={{0,4},{1,5},{2,6},{3,7},{4,8},{5,9},{6,10},{7,11},{8,12},{9,13},{1... | collective-permute-start | bytes 392 | tf_op jit(solution)/shard_map/ppermute | solution.py:34
  215.9 4.4 collective-permute-start.24
  221.6 5.2 collective-permute-start.22
  231.7 20.3 %fusion.411 = (f32[1,2,16,1,64,1]{0,5,4,3,2,1:T(1,128)S(1)}, f32[1,2,16,1,64,1]{0,5,4,3,2,1:T(1,128)S(1)}, f32[1,2,16,1,64,1]{0,5,4,3,2,1:T(1,128)}, f32[1,2,16,...) fusion(f32[7,2,16,2,64,2]{0,5,4,3,2,1:T(2,128)} %bitcast.228), kind=kLoop, calls=%fused_computation.732 | loop fusion | bytes 131072 | tf_op jit(solution)/shard_map/slice | solution.py:82
  286.6 5.2 collective-permute-start.28
  304.4 5.5 collective-permute-start.30
  311.9 7.1 collective-permute-done.31
  321.7 6.3 collective-permute-start.36
  329.2 5.2 collective-permute-start.34
  339.6 8.2 %collective-permute-start.40 = (f32[2,16,1]{2,1,0:T(8,128)S(1)}, f32[2,16,1]{2,1,0:T(8,128)S(1)}, u32[]{:S(2)}, u32[]{:S(2)}) collective-permute-start(f32[2,16,1]{2,1,0:T(8,128)S(1)} %get-tuple-element.216), channel_id=1, source_target_pairs={{0,4},{1,5},{2,6},{3,7},{4,8},{5,9},{6,10},{7,11},{8,12},{9,13},{1... | collective-permute-start | bytes 392 | tf_op jit(solution)/shard_map/ppermute | solution.py:34
  356.4 8.2 %collective-permute-start.44 = (f32[2,16,1]{2,1,0:T(8,128)S(1)}, f32[2,16,1]{2,1,0:T(8,128)S(1)}, u32[]{:S(2)}, u32[]{:S(2)}) collective-permute-start(f32[2,16,1]{2,1,0:T(8,128)S(1)} %get-tuple-element.208), channel_id=1, source_target_pairs={{0,4},{1,5},{2,6},{3,7},{4,8},{5,9},{6,10},{7,11},{8,12},{9,13},{1... | collective-permute-start | bytes 392 | tf_op jit(solution)/shard_map/ppermute | solution.py:34
  385.7 7.8 %collective-permute-start.52 = (f32[2,32,1]{2,1,0:T(8,128)S(1)}, f32[2,32,1]{2,1,0:T(8,128)S(1)}, u32[]{:S(2)}, u32[]{:S(2)}) collective-permute-start(f32[2,32,1]{2,1,0:T(8,128)S(1)} %get-tuple-element.146), channel_id=1, source_target_pairs={{0,2},{1,3},{2,4},{3,5},{4,6},{5,7},{6,8},{7,9},{8,10},{9,11},{10,... | collective-permute-start | bytes 776 | tf_op jit(solution)/shard_map/ppermute | solution.py:34
  412.7 7.0 collective-permute-done.57
  433.8 4.6 collective-permute-start.60
  439.8 5.5 collective-permute-done.61
  445.3 4.2 fusion.10
  449.6 5.1 collective-permute-start.64
  482.8 4.3 collective-permute-done.71
  487.2 5.8 reshape.250
  501.0 4.2 collective-permute-start.75
  506.5 4.6 collective-permute-start.73
  516.2 5.2 collective-permute-start.79
  532.4 5.2 collective-permute-start.81
  538.9 7.6 %collective-permute-start.84 = (f32[2,16,1]{2,1,0:T(8,128)S(1)}, f32[2,16,1]{2,1,0:T(8,128)S(1)}, u32[]{:S(2)}, u32[]{:S(2)}) collective-permute-start(f32[2,16,1]{2,1,0:T(8,128)S(1)} %get-tuple-element.198), channel_id=1, source_target_pairs={{0,4},{1,5},{2,6},{3,7},{4,8},{5,9},{6,10},{7,11},{8,12},{9,13},{1... | collective-permute-start | bytes 392 | tf_op jit(solution)/shard_map/ppermute | solution.py:34
  556.3 8.2 %collective-permute-start.88 = (f32[2,16,1]{2,1,0:T(8,128)S(1)}, f32[2,16,1]{2,1,0:T(8,128)S(1)}, u32[]{:S(2)}, u32[]{:S(2)}) collective-permute-start(f32[2,16,1]{2,1,0:T(8,128)S(1)} %get-tuple-element.190), channel_id=1, source_target_pairs={{0,4},{1,5},{2,6},{3,7},{4,8},{5,9},{6,10},{7,11},{8,12},{9,13},{1... | collective-permute-start | bytes 392 | tf_op jit(solution)/shard_map/ppermute | solution.py:34
  573.3 8.0 %collective-permute-start.92 = (f32[2,16,1]{2,1,0:T(8,128)S(1)}, f32[2,16,1]{2,1,0:T(8,128)S(1)}, u32[]{:S(2)}, u32[]{:S(2)}) collective-permute-start(f32[2,16,1]{2,1,0:T(8,128)S(1)} %get-tuple-element.182), channel_id=1, source_target_pairs={{0,4},{1,5},{2,6},{3,7},{4,8},{5,9},{6,10},{7,11},{8,12},{9,13},{1... | collective-permute-start | bytes 392 | tf_op jit(solution)/shard_map/ppermute | solution.py:34
  602.4 7.6 %collective-permute-start.100 = (f32[2,32,1]{2,1,0:T(8,128)S(1)}, f32[2,32,1]{2,1,0:T(8,128)S(1)}, u32[]{:S(2)}, u32[]{:S(2)}) collective-permute-start(f32[2,32,1]{2,1,0:T(8,128)S(1)} %get-tuple-element.110), channel_id=1, source_target_pairs={{0,2},{1,3},{2,4},{3,5},{4,6},{5,7},{6,8},{7,9},{8,10},{9,11},{10,... | collective-permute-start | bytes 776 | tf_op jit(solution)/shard_map/ppermute | solution.py:34
  630.8 5.6 collective-permute-done.105
  649.6 4.9 collective-permute-done.109
  662.9 4.9 collective-permute-start.112
  675.0 49.4 %all-reduce.41.cloned.1.call-done = f32[2,64,128]{2,1,0:T(8,128)} async-done(((f32[2,64,128]{2,1,0:T(8,128)}), f32[2,64,128]{2,1,0:T(8,128)}) %all-reduce.41.cloned.1.call-update) | async-done | bytes 65552 | tf_op jit(solution)/shard_map/psum | solution.py:282
  (556 shorter events, 380.4 us)
Async XLA Ops:
  7.2 717.3 %all-reduce.41.cloned.1.call-start = ((), (), s32[]{:S(2)}) async-start(), calls=%async_computation | async-start | bytes 131072 | tf_op jit(solution)/shard_map/psum | solution.py:282
  12.1 32.8 %collective-permute-start = (f32[2,1,128]{2,1,0:T(1,128)S(1)}, f32[2,1,128]{2,1,0:T(1,128)S(1)}, u32[]{:S(2)}, u32[]{:S(2)}) collective-permute-start(f32[2,1,128]{2,1,0:T(1,128)S(1)} %get-tuple-element.102), channel_id=1, source_target_pairs={{0,16},{16,32},{32,48},{48,64},{64,80},{80,96},{96,112},{1,17},{17... | collective-permute-start | bytes 3080 | tf_op jit(solution)/shard_map/ppermute | solution.py:23
  16.7 28.2 %collective-permute-start.1 = (f32[2,1,128]{2,1,0:T(1,128)S(1)}, f32[2,1,128]{2,1,0:T(1,128)S(1)}, u32[]{:S(2)}, u32[]{:S(2)}) collective-permute-start(f32[2,1,128]{2,1,0:T(1,128)S(1)} %get-tuple-element.101), channel_id=1, source_target_pairs={{16,0},{32,16},{48,32},{64,48},{80,64},{96,80},{112,96},{17,1},{33... | collective-permute-start | bytes 3080 | tf_op jit(solution)/shard_map/ppermute | solution.py:26
  22.9 25.2 %collective-permute-start.4 = (f32[2,1,128]{2,1,0:T(1,128)S(1)}, f32[2,1,128]{2,1,0:T(1,128)S(1)}, u32[]{:S(2)}, u32[]{:S(2)}) collective-permute-start(f32[2,1,128]{2,1,0:T(1,128)S(1)} %get-tuple-element.103), channel_id=1, source_target_pairs={{0,16},{16,32},{32,48},{48,64},{64,80},{80,96},{96,112},{1,17},{17... | collective-permute-start | bytes 3080 | tf_op jit(solution)/shard_map/ppermute | solution.py:23
  24.8 23.2 %collective-permute-start.5 = (f32[2,1,128]{2,1,0:T(1,128)S(1)}, f32[2,1,128]{2,1,0:T(1,128)S(1)}, u32[]{:S(2)}, u32[]{:S(2)}) collective-permute-start(f32[2,1,128]{2,1,0:T(1,128)S(1)} %get-tuple-element.104), channel_id=1, source_target_pairs={{16,0},{32,16},{48,32},{64,48},{80,64},{96,80},{112,96},{17,1},{33... | collective-permute-start | bytes 3080 | tf_op jit(solution)/shard_map/ppermute | solution.py:26
  27.8 183.3 %collective-permute-start.18 = (f32[2,1,128]{2,1,0:T(1,128)}, f32[2,1,128]{2,1,0:T(1,128)}, u32[]{:S(2)}, u32[]{:S(2)}) collective-permute-start(f32[2,1,128]{2,1,0:T(1,128)} %broadcast.180), channel_id=1, source_target_pairs={{0,16},{16,32},{32,48},{48,64},{64,80},{80,96},{96,112},{1,17},{17... | collective-permute-start | bytes 3080 | tf_op jit(solution)/shard_map/ppermute | solution.py:34
  45.1 18.6 %collective-permute-start.2 = (f32[2,66,1]{2,1,0:T(8,128)S(1)}, f32[2,66,1]{2,1,0:T(8,128)S(1)}, u32[]{:S(2)}, u32[]{:S(2)}) collective-permute-start(f32[2,66,1]{2,1,0:T(8,128)S(1)} %get-tuple-element.78), channel_id=1, source_target_pairs={{0,1},{1,2},{2,3},{3,4},{4,5},{5,6},{6,7},{7,8},{8,9},{9,10},{10,1... | collective-permute-start | bytes 1592 | tf_op jit(solution)/shard_map/ppermute | solution.py:23
  46.8 18.8 %collective-permute-start.3 = (f32[2,66,1]{2,1,0:T(8,128)S(1)}, f32[2,66,1]{2,1,0:T(8,128)S(1)}, u32[]{:S(2)}, u32[]{:S(2)}) collective-permute-start(f32[2,66,1]{2,1,0:T(8,128)S(1)} %get-tuple-element.77), channel_id=1, source_target_pairs={{1,0},{2,1},{3,2},{4,3},{5,4},{6,5},{7,6},{8,7},{9,8},{10,9},{11,1... | collective-permute-start | bytes 1592 | tf_op jit(solution)/shard_map/ppermute | solution.py:26
  49.0 23.4 %collective-permute-start.6 = (f32[2,66,1]{2,1,0:T(8,128)S(1)}, f32[2,66,1]{2,1,0:T(8,128)S(1)}, u32[]{:S(2)}, u32[]{:S(2)}) collective-permute-start(f32[2,66,1]{2,1,0:T(8,128)S(1)} %get-tuple-element.79), channel_id=1, source_target_pairs={{0,1},{1,2},{2,3},{3,4},{4,5},{5,6},{6,7},{7,8},{8,9},{9,10},{10,1... | collective-permute-start | bytes 1592 | tf_op jit(solution)/shard_map/ppermute | solution.py:23
  53.2 19.2 %collective-permute-start.7 = (f32[2,66,1]{2,1,0:T(8,128)S(1)}, f32[2,66,1]{2,1,0:T(8,128)S(1)}, u32[]{:S(2)}, u32[]{:S(2)}) collective-permute-start(f32[2,66,1]{2,1,0:T(8,128)S(1)} %get-tuple-element.80), channel_id=1, source_target_pairs={{1,0},{2,1},{3,2},{4,3},{5,4},{6,5},{7,6},{8,7},{9,8},{10,9},{11,1... | collective-permute-start | bytes 1592 | tf_op jit(solution)/shard_map/ppermute | solution.py:26
  63.7 147.5 %collective-permute-start.19 = (f32[2,1,128]{2,1,0:T(1,128)}, f32[2,1,128]{2,1,0:T(1,128)}, u32[]{:S(2)}, u32[]{:S(2)}) collective-permute-start(f32[2,1,128]{2,1,0:T(1,128)} %broadcast.180), channel_id=1, source_target_pairs={{16,0},{32,16},{48,32},{64,48},{80,64},{96,80},{112,96},{17,1},{33... | collective-permute-start | bytes 3080 | tf_op jit(solution)/shard_map/ppermute | solution.py:34
  65.6 145.5 %collective-permute-start.20 = (f32[2,32,1]{2,1,0:T(8,128)S(1)}, f32[2,32,1]{2,1,0:T(8,128)S(1)}, u32[]{:S(2)}, u32[]{:S(2)}) collective-permute-start(f32[2,32,1]{2,1,0:T(8,128)S(1)} %broadcast.181), channel_id=1, source_target_pairs={{0,2},{1,3},{2,4},{3,5},{4,6},{5,7},{6,8},{7,9},{8,10},{9,11},{10,... | collective-permute-start | bytes 776 | tf_op jit(solution)/shard_map/ppermute | solution.py:34
  76.0 54.4 %collective-permute-start.8 = (f32[2,1,128]{2,1,0:T(1,128)S(1)}, f32[2,1,128]{2,1,0:T(1,128)S(1)}, u32[]{:S(2)}, u32[]{:S(2)}) collective-permute-start(f32[2,1,128]{2,1,0:T(1,128)S(1)} %get-tuple-element.99), channel_id=1, source_target_pairs={{0,16},{16,32},{32,48},{48,64},{64,80},{80,96},{96,112},{1,17},{17... | collective-permute-start | bytes 3080 | tf_op jit(solution)/shard_map/ppermute | solution.py:23
  79.9 50.4 %collective-permute-start.9 = (f32[2,1,128]{2,1,0:T(1,128)S(1)}, f32[2,1,128]{2,1,0:T(1,128)S(1)}, u32[]{:S(2)}, u32[]{:S(2)}) collective-permute-start(f32[2,1,128]{2,1,0:T(1,128)S(1)} %get-tuple-element.100), channel_id=1, source_target_pairs={{16,0},{32,16},{48,32},{64,48},{80,64},{96,80},{112,96},{17,1},{33... | collective-permute-start | bytes 3080 | tf_op jit(solution)/shard_map/ppermute | solution.py:26
  130.5 14.5 %collective-permute-start.10 = (f32[2,66,1]{2,1,0:T(8,128)S(1)}, f32[2,66,1]{2,1,0:T(8,128)S(1)}, u32[]{:S(2)}, u32[]{:S(2)}) collective-permute-start(f32[2,66,1]{2,1,0:T(8,128)S(1)} %get-tuple-element.73), channel_id=1, source_target_pairs={{0,1},{1,2},{2,3},{3,4},{4,5},{5,6},{6,7},{7,8},{8,9},{9,10},{10,1... | collective-permute-start | bytes 1592 | tf_op jit(solution)/shard_map/ppermute | solution.py:23
  135.0 9.9 %collective-permute-start.11 = (f32[2,66,1]{2,1,0:T(8,128)S(1)}, f32[2,66,1]{2,1,0:T(8,128)S(1)}, u32[]{:S(2)}, u32[]{:S(2)}) collective-permute-start(f32[2,66,1]{2,1,0:T(8,128)S(1)} %get-tuple-element.74), channel_id=1, source_target_pairs={{1,0},{2,1},{3,2},{4,3},{5,4},{6,5},{7,6},{8,7},{9,8},{10,9},{11,1... | collective-permute-start | bytes 1592 | tf_op jit(solution)/shard_map/ppermute | solution.py:26
  149.2 14.2 %collective-permute-start.12 = (f32[2,1,128]{2,1,0:T(1,128)S(1)}, f32[2,1,128]{2,1,0:T(1,128)S(1)}, u32[]{:S(2)}, u32[]{:S(2)}) collective-permute-start(f32[2,1,128]{2,1,0:T(1,128)S(1)} %get-tuple-element.97), channel_id=1, source_target_pairs={{0,16},{16,32},{32,48},{48,64},{64,80},{80,96},{96,112},{1,17},{17... | collective-permute-start | bytes 3080 | tf_op jit(solution)/shard_map/ppermute | solution.py:23
  153.2 10.3 %collective-permute-start.13 = (f32[2,1,128]{2,1,0:T(1,128)S(1)}, f32[2,1,128]{2,1,0:T(1,128)S(1)}, u32[]{:S(2)}, u32[]{:S(2)}) collective-permute-start(f32[2,1,128]{2,1,0:T(1,128)S(1)} %get-tuple-element.98), channel_id=1, source_target_pairs={{16,0},{32,16},{48,32},{64,48},{80,64},{96,80},{112,96},{17,1},{33... | collective-permute-start | bytes 3080 | tf_op jit(solution)/shard_map/ppermute | solution.py:26
  170.2 40.9 %collective-permute-start.21 = (f32[2,32,1]{2,1,0:T(8,128)S(1)}, f32[2,32,1]{2,1,0:T(8,128)S(1)}, u32[]{:S(2)}, u32[]{:S(2)}) collective-permute-start(f32[2,32,1]{2,1,0:T(8,128)S(1)} %broadcast.181), channel_id=1, source_target_pairs={{2,0},{3,1},{4,2},{5,3},{6,4},{7,5},{8,6},{9,7},{10,8},{11,9},{12,... | collective-permute-start | bytes 776 | tf_op jit(solution)/shard_map/ppermute | solution.py:34
  190.8 9.2 %collective-permute-start.17 = (f32[7,2,32,64]{3,2,1,0:T(8,128)S(1)}, f32[7,2,32,64]{3,2,1,0:T(8,128)S(1)}, u32[]{:S(2)}, u32[]{:S(2)}) collective-permute-start(f32[7,2,32,64]{3,2,1,0:T(8,128)S(1)} %bitcast_dynamic-update-slice_fusion.1), channel_id=1, source_target_pairs={{0,1},{1,0},{2,3},{3,2},{4,5},{5,4},{6,7},{7,6},{8,9},{9,8},{10,11... | collective-permute-start | bytes 344072 | tf_op jit(solution)/shard_map/ppermute | solution.py:38
  200.6 119.4 %collective-permute-start.32 = (f32[2,16,1]{2,1,0:T(8,128)}, f32[2,16,1]{2,1,0:T(8,128)}, u32[]{:S(2)}, u32[]{:S(2)}) collective-permute-start(f32[2,16,1]{2,1,0:T(8,128)} %broadcast.184), channel_id=1, source_target_pairs={{0,4},{1,5},{2,6},{3,7},{4,8},{5,9},{6,10},{7,11},{8,12},{9,13},{1... | collective-permute-start | bytes 392 | tf_op jit(solution)/shard_map/ppermute | solution.py:34
  215.9 69.6 %collective-permute-start.24 = (f32[2,32,1]{2,1,0:T(8,128)}, f32[2,32,1]{2,1,0:T(8,128)}, u32[]{:S(2)}, u32[]{:S(2)}) collective-permute-start(f32[2,32,1]{2,1,0:T(8,128)} %get-tuple-element.172), channel_id=1, source_target_pairs={{0,2},{1,3},{2,4},{3,5},{4,6},{5,7},{6,8},{7,9},{8,10},{9,11},{10,... | collective-permute-start | bytes 776 | tf_op jit(solution)/shard_map/ppermute | solution.py:34
  220.3 65.2 %collective-permute-start.25 = (f32[2,32,1]{2,1,0:T(8,128)}, f32[2,32,1]{2,1,0:T(8,128)}, u32[]{:S(2)}, u32[]{:S(2)}) collective-permute-start(f32[2,32,1]{2,1,0:T(8,128)} %get-tuple-element.171), channel_id=1, source_target_pairs={{2,0},{3,1},{4,2},{5,3},{6,4},{7,5},{8,6},{9,7},{10,8},{11,9},{12,... | collective-permute-start | bytes 776 | tf_op jit(solution)/shard_map/ppermute | solution.py:34
  221.6 63.9 %collective-permute-start.22 = (f32[2,1,128]{2,1,0:T(1,128)}, f32[2,1,128]{2,1,0:T(1,128)}, u32[]{:S(2)}, u32[]{:S(2)}) collective-permute-start(f32[2,1,128]{2,1,0:T(1,128)} %get-tuple-element.176), channel_id=1, source_target_pairs={{0,16},{16,32},{32,48},{48,64},{64,80},{80,96},{96,112},{1,17},{17... | collective-permute-start | bytes 3080 | tf_op jit(solution)/shard_map/ppermute | solution.py:34
  226.8 58.7 %collective-permute-start.23 = (f32[2,1,128]{2,1,0:T(1,128)}, f32[2,1,128]{2,1,0:T(1,128)}, u32[]{:S(2)}, u32[]{:S(2)}) collective-permute-start(f32[2,1,128]{2,1,0:T(1,128)} %get-tuple-element.175), channel_id=1, source_target_pairs={{16,0},{32,16},{48,32},{64,48},{80,64},{96,80},{112,96},{17,1},{33... | collective-permute-start | bytes 3080 | tf_op jit(solution)/shard_map/ppermute | solution.py:34
  286.6 12.3 %collective-permute-start.28 = (f32[2,32,1]{2,1,0:T(8,128)S(1)}, f32[2,32,1]{2,1,0:T(8,128)S(1)}, u32[]{:S(2)}, u32[]{:S(2)}) collective-permute-start(f32[2,32,1]{2,1,0:T(8,128)S(1)} %get-tuple-element.164), channel_id=1, source_target_pairs={{0,2},{1,3},{2,4},{3,5},{4,6},{5,7},{6,8},{7,9},{8,10},{9,11},{10,... | collective-permute-start | bytes 776 | tf_op jit(solution)/shard_map/ppermute | solution.py:34
  299.0 21.1 %collective-permute-start.33 = (f32[2,16,1]{2,1,0:T(8,128)}, f32[2,16,1]{2,1,0:T(8,128)S(1)}, u32[]{:S(2)}, u32[]{:S(2)}) collective-permute-start(f32[2,16,1]{2,1,0:T(8,128)} %broadcast.184), channel_id=1, source_target_pairs={{4,0},{5,1},{6,2},{7,3},{8,4},{9,5},{10,6},{11,7},{12,8},{13,9},{1... | collective-permute-start | bytes 392 | tf_op jit(solution)/shard_map/ppermute | solution.py:34
  310.0 9.0 %collective-permute-start.31 = (f32[7,2,16,64]{3,2,1,0:T(8,128)S(1)}, f32[7,2,16,64]{3,2,1,0:T(8,128)S(1)}, u32[]{:S(2)}, u32[]{:S(2)}) collective-permute-start(f32[7,2,16,64]{3,2,1,0:T(8,128)S(1)} %constant_dynamic-update-slice_fusion), channel_id=1, source_target_pairs={{0,2},{1,3},{2,0},{3,1},{4,6},{5,7},{6,4},{7,5},{8,10},{9,11},{10,... | collective-permute-start | bytes 172040 | tf_op jit(solution)/shard_map/ppermute | solution.py:38
  321.7 14.7 %collective-permute-start.36 = (f32[2,16,1]{2,1,0:T(8,128)S(1)}, f32[2,16,1]{2,1,0:T(8,128)S(1)}, u32[]{:S(2)}, u32[]{:S(2)}) collective-permute-start(f32[2,16,1]{2,1,0:T(8,128)S(1)} %get-tuple-element.224), channel_id=1, source_target_pairs={{0,4},{1,5},{2,6},{3,7},{4,8},{5,9},{6,10},{7,11},{8,12},{9,13},{1... | collective-permute-start | bytes 392 | tf_op jit(solution)/shard_map/ppermute | solution.py:34
  339.6 13.8 %collective-permute-start.40 = (f32[2,16,1]{2,1,0:T(8,128)S(1)}, f32[2,16,1]{2,1,0:T(8,128)S(1)}, u32[]{:S(2)}, u32[]{:S(2)}) collective-permute-start(f32[2,16,1]{2,1,0:T(8,128)S(1)} %get-tuple-element.216), channel_id=1, source_target_pairs={{0,4},{1,5},{2,6},{3,7},{4,8},{5,9},{6,10},{7,11},{8,12},{9,13},{1... | collective-permute-start | bytes 392 | tf_op jit(solution)/shard_map/ppermute | solution.py:34
  356.4 13.8 %collective-permute-start.44 = (f32[2,16,1]{2,1,0:T(8,128)S(1)}, f32[2,16,1]{2,1,0:T(8,128)S(1)}, u32[]{:S(2)}, u32[]{:S(2)}) collective-permute-start(f32[2,16,1]{2,1,0:T(8,128)S(1)} %get-tuple-element.208), channel_id=1, source_target_pairs={{0,4},{1,5},{2,6},{3,7},{4,8},{5,9},{6,10},{7,11},{8,12},{9,13},{1... | collective-permute-start | bytes 392 | tf_op jit(solution)/shard_map/ppermute | solution.py:34
  375.1 10.4 %collective-permute-start.49 = (f32[2,32,1]{2,1,0:T(8,128)S(1)}, f32[2,32,1]{2,1,0:T(8,128)S(1)}, u32[]{:S(2)}, u32[]{:S(2)}) collective-permute-start(f32[2,32,1]{2,1,0:T(8,128)S(1)} %get-tuple-element.153), channel_id=1, source_target_pairs={{2,0},{3,1},{4,2},{5,3},{6,4},{7,5},{8,6},{9,7},{10,8},{11,9},{12,... | collective-permute-start | bytes 776 | tf_op jit(solution)/shard_map/ppermute | solution.py:34
  376.4 9.1 %collective-permute-start.46 = (f32[2,1,128]{2,1,0:T(1,128)S(1)}, f32[2,1,128]{2,1,0:T(1,128)S(1)}, u32[]{:S(2)}, u32[]{:S(2)}) collective-permute-start(f32[2,1,128]{2,1,0:T(1,128)S(1)} %get-tuple-element.158), channel_id=1, source_target_pairs={{0,16},{16,32},{32,48},{48,64},{64,80},{80,96},{96,112},{1,17},{17... | collective-permute-start | bytes 3080 | tf_op jit(solution)/shard_map/ppermute | solution.py:34
  385.7 13.4 %collective-permute-start.52 = (f32[2,32,1]{2,1,0:T(8,128)S(1)}, f32[2,32,1]{2,1,0:T(8,128)S(1)}, u32[]{:S(2)}, u32[]{:S(2)}) collective-permute-start(f32[2,32,1]{2,1,0:T(8,128)S(1)} %get-tuple-element.146), channel_id=1, source_target_pairs={{0,2},{1,3},{2,4},{3,5},{4,6},{5,7},{6,8},{7,9},{8,10},{9,11},{10,... | collective-permute-start | bytes 776 | tf_op jit(solution)/shard_map/ppermute | solution.py:34
  410.7 9.0 %collective-permute-start.57 = (f32[2,66,1]{2,1,0:T(8,128)S(1)}, f32[2,66,1]{2,1,0:T(8,128)S(1)}, u32[]{:S(2)}, u32[]{:S(2)}) collective-permute-start(f32[2,66,1]{2,1,0:T(8,128)S(1)} %get-tuple-element.70), channel_id=1, source_target_pairs={{1,0},{2,1},{3,2},{4,3},{5,4},{6,5},{7,6},{8,7},{9,8},{10,9},{11,1... | collective-permute-start | bytes 1592 | tf_op jit(solution)/shard_map/ppermute | solution.py:26
  423.2 10.5 %collective-permute-start.58 = (f32[2,1,128]{2,1,0:T(1,128)S(1)}, f32[2,1,128]{2,1,0:T(1,128)S(1)}, u32[]{:S(2)}, u32[]{:S(2)}) collective-permute-start(f32[2,1,128]{2,1,0:T(1,128)S(1)} %get-tuple-element.91), channel_id=1, source_target_pairs={{0,16},{16,32},{32,48},{48,64},{64,80},{80,96},{96,112},{1,17},{17... | collective-permute-start | bytes 3080 | tf_op jit(solution)/shard_map/ppermute | solution.py:23
  428.4 11.3 %collective-permute-start.62 = (f32[2,66,1]{2,1,0:T(8,128)S(1)}, f32[2,66,1]{2,1,0:T(8,128)S(1)}, u32[]{:S(2)}, u32[]{:S(2)}) collective-permute-start(f32[2,66,1]{2,1,0:T(8,128)S(1)} %get-tuple-element.75), channel_id=1, source_target_pairs={{0,1},{1,2},{2,3},{3,4},{4,5},{5,6},{6,7},{7,8},{8,9},{9,10},{10,1... | collective-permute-start | bytes 1592 | tf_op jit(solution)/shard_map/ppermute | solution.py:23
  501.0 12.0 %collective-permute-start.75 = (f32[2,32,1]{2,1,0:T(8,128)S(1)}, f32[2,32,1]{2,1,0:T(8,128)S(1)}, u32[]{:S(2)}, u32[]{:S(2)}) collective-permute-start(f32[2,32,1]{2,1,0:T(8,128)S(1)} %get-tuple-element.136), channel_id=1, source_target_pairs={{0,2},{1,3},{2,4},{3,5},{4,6},{5,7},{6,8},{7,9},{8,10},{9,11},{10,... | collective-permute-start | bytes 776 | tf_op jit(solution)/shard_map/ppermute | solution.py:34
  516.2 10.8 %collective-permute-start.79 = (f32[2,32,1]{2,1,0:T(8,128)S(1)}, f32[2,32,1]{2,1,0:T(8,128)S(1)}, u32[]{:S(2)}, u32[]{:S(2)}) collective-permute-start(f32[2,32,1]{2,1,0:T(8,128)S(1)} %get-tuple-element.128), channel_id=1, source_target_pairs={{0,2},{1,3},{2,4},{3,5},{4,6},{5,7},{6,8},{7,9},{8,10},{9,11},{10,... | collective-permute-start | bytes 776 | tf_op jit(solution)/shard_map/ppermute | solution.py:34
  538.9 14.2 %collective-permute-start.84 = (f32[2,16,1]{2,1,0:T(8,128)S(1)}, f32[2,16,1]{2,1,0:T(8,128)S(1)}, u32[]{:S(2)}, u32[]{:S(2)}) collective-permute-start(f32[2,16,1]{2,1,0:T(8,128)S(1)} %get-tuple-element.198), channel_id=1, source_target_pairs={{0,4},{1,5},{2,6},{3,7},{4,8},{5,9},{6,10},{7,11},{8,12},{9,13},{1... | collective-permute-start | bytes 392 | tf_op jit(solution)/shard_map/ppermute | solution.py:34
  546.5 8.9 %collective-permute-start.85 = (f32[2,16,1]{2,1,0:T(8,128)S(1)}, f32[2,16,1]{2,1,0:T(8,128)S(1)}, u32[]{:S(2)}, u32[]{:S(2)}) collective-permute-start(f32[2,16,1]{2,1,0:T(8,128)S(1)} %get-tuple-element.197), channel_id=1, source_target_pairs={{4,0},{5,1},{6,2},{7,3},{8,4},{9,5},{10,6},{11,7},{12,8},{13,9},{1... | collective-permute-start | bytes 392 | tf_op jit(solution)/shard_map/ppermute | solution.py:34
  556.3 13.8 %collective-permute-start.88 = (f32[2,16,1]{2,1,0:T(8,128)S(1)}, f32[2,16,1]{2,1,0:T(8,128)S(1)}, u32[]{:S(2)}, u32[]{:S(2)}) collective-permute-start(f32[2,16,1]{2,1,0:T(8,128)S(1)} %get-tuple-element.190), channel_id=1, source_target_pairs={{0,4},{1,5},{2,6},{3,7},{4,8},{5,9},{6,10},{7,11},{8,12},{9,13},{1... | collective-permute-start | bytes 392 | tf_op jit(solution)/shard_map/ppermute | solution.py:34
  564.5 8.6 %collective-permute-start.89 = (f32[2,16,1]{2,1,0:T(8,128)S(1)}, f32[2,16,1]{2,1,0:T(8,128)S(1)}, u32[]{:S(2)}, u32[]{:S(2)}) collective-permute-start(f32[2,16,1]{2,1,0:T(8,128)S(1)} %get-tuple-element.189), channel_id=1, source_target_pairs={{4,0},{5,1},{6,2},{7,3},{8,4},{9,5},{10,6},{11,7},{12,8},{13,9},{1... | collective-permute-start | bytes 392 | tf_op jit(solution)/shard_map/ppermute | solution.py:34
  573.3 13.7 %collective-permute-start.92 = (f32[2,16,1]{2,1,0:T(8,128)S(1)}, f32[2,16,1]{2,1,0:T(8,128)S(1)}, u32[]{:S(2)}, u32[]{:S(2)}) collective-permute-start(f32[2,16,1]{2,1,0:T(8,128)S(1)} %get-tuple-element.182), channel_id=1, source_target_pairs={{0,4},{1,5},{2,6},{3,7},{4,8},{5,9},{6,10},{7,11},{8,12},{9,13},{1... | collective-permute-start | bytes 392 | tf_op jit(solution)/shard_map/ppermute | solution.py:34
  581.3 8.6 %collective-permute-start.93 = (f32[2,16,1]{2,1,0:T(8,128)S(1)}, f32[2,16,1]{2,1,0:T(8,128)S(1)}, u32[]{:S(2)}, u32[]{:S(2)}) collective-permute-start(f32[2,16,1]{2,1,0:T(8,128)S(1)} %get-tuple-element.181), channel_id=1, source_target_pairs={{4,0},{5,1},{6,2},{7,3},{8,4},{9,5},{10,6},{11,7},{12,8},{13,9},{1... | collective-permute-start | bytes 392 | tf_op jit(solution)/shard_map/ppermute | solution.py:34
  590.5 8.6 %collective-permute-start.96 = (f32[2,32,1]{2,1,0:T(8,128)S(1)}, f32[2,32,1]{2,1,0:T(8,128)S(1)}, u32[]{:S(2)}, u32[]{:S(2)}) collective-permute-start(f32[2,32,1]{2,1,0:T(8,128)S(1)} %get-tuple-element.118), channel_id=1, source_target_pairs={{0,2},{1,3},{2,4},{3,5},{4,6},{5,7},{6,8},{7,9},{8,10},{9,11},{10,... | collective-permute-start | bytes 776 | tf_op jit(solution)/shard_map/ppermute | solution.py:34
  592.4 9.8 %collective-permute-start.97 = (f32[2,32,1]{2,1,0:T(8,128)S(1)}, f32[2,32,1]{2,1,0:T(8,128)S(1)}, u32[]{:S(2)}, u32[]{:S(2)}) collective-permute-start(f32[2,32,1]{2,1,0:T(8,128)S(1)} %get-tuple-element.117), channel_id=1, source_target_pairs={{2,0},{3,1},{4,2},{5,3},{6,4},{7,5},{8,6},{9,7},{10,8},{11,9},{12,... | collective-permute-start | bytes 776 | tf_op jit(solution)/shard_map/ppermute | solution.py:34
  602.4 13.3 %collective-permute-start.100 = (f32[2,32,1]{2,1,0:T(8,128)S(1)}, f32[2,32,1]{2,1,0:T(8,128)S(1)}, u32[]{:S(2)}, u32[]{:S(2)}) collective-permute-start(f32[2,32,1]{2,1,0:T(8,128)S(1)} %get-tuple-element.110), channel_id=1, source_target_pairs={{0,2},{1,3},{2,4},{3,5},{4,6},{5,7},{6,8},{7,9},{8,10},{9,11},{10,... | collective-permute-start | bytes 776 | tf_op jit(solution)/shard_map/ppermute | solution.py:34
  (136 other events, 3220.0 us)
Sparse Core Ops, SparseCore 0:
  675.2 49.2 all-reduce.40
where the time goes:
time: 743 us; the launch traced here: 733 us
  starting transfers between devices  345 us (46%)
  waiting for transfers between devices  159 us (21%)
  local copies, waits for them, and re-layouts  146 us (20%)
  other arithmetic  65.3 us (9%)
  between operations  17.6 us (2%)
    ppermute x62, starting transfers between devices, passed_along(): lax.ppermute(value, axis, [(source, source + steps) for source in range(f...  199 us
    ppermute x23, starting transfers between devices, extended(): lax.ppermute(lax.slice_in_dim(block, block.shape[dim] - width, None, axis...  81.4 us
    ppermute x23, waiting for transfers between devices, extended(): lax.ppermute(lax.slice_in_dim(block, 0, width, axis=dim), axis, backward)  54.9 us
    psum x1, waiting for transfers between devices, shards(): gradient = lax.psum(-local_terms, 'scen')  49.4 us
    ppermute x23, starting transfers between devices, extended(): lax.ppermute(lax.slice_in_dim(block, 0, width, axis=dim), axis, backward)  42.3 us
    ppermute x62, waiting for transfers between devices, passed_along(): lax.ppermute(value, axis, [(source, source + steps) for source in range(f...  36.8 us
    unnamed x158, local copies, waits for them, and re-layouts  34.5 us
    slice x2, local copies, waits for them, and re-layouts, coarsen(): quads[3, :, :, 1, :, 1]  25 us
  transfers between devices with their start and end apart: 115, of which 44 were waited for; matrix products, arithmetic and copies ran while one was open for 24% of the time, Pallas kernels for 0%

commit v1 on v0

v1 whole, which is shorter than its diff:
```python
from functools import partial

import jax
import jax.numpy as jnp
from jax import lax
from jax.experimental import pallas as pl
from jax.experimental.pallas import tpu as pltpu
from jax.sharding import PartitionSpec as P

WELLS = 5
FACIES = 4
VERTICAL = 0.3
DAMPING = 0.8
ROWS = 64
LANES = 128
HALO = 32
GUARD = 8
MESH = pl.DeviceIdType.MESH

TOP = (GUARD + HALO, GUARD + HALO // 2, GUARD + HALO // 4)
HEIGHT = tuple(ROWS // 2**k + 2 * TOP[k] for k in range(3))
CHUNK = 16


def over(level, low, high, body, step=CHUNK):
    base = TOP[level]
    for row in range(low, high, step):
        body(base + row, min(step, high - row))


def lanes_of(count):
    return lax.broadcasted_iota(jnp.int32, (count, LANES), 1)


def turn(value, shift):
    return pltpu.roll(value, shift % LANES, 1)


def to_right(m0, m1, h, hs, m1s, lane, s):
    return (
        turn(jnp.where(lane < s, h, m0), -s),
        turn(jnp.where(lane < s, hs, m1), -s),
        turn(jnp.where(lane < s, m0, jnp.where((lane >= 64) & (lane < 64 + s), m1s, h)), -s),
    )


def to_left(m0, m1, h, hs, m1s, lane, s):
    return (
        turn(jnp.where(lane >= LANES - s, h, m0), s),
        turn(jnp.where(lane >= LANES - s, hs, m1), s),
        turn(jnp.where(lane >= LANES - s, m0, jnp.where((lane >= 64 - s) & (lane < 64), m1s, h)), s),
    )


def tiles(ref, row, count):
    return tuple(ref[t, pl.ds(row, count), :] for t in range(3))


def change(v, g, e, level, row, count):
    s = 2**level
    lane = lanes_of(count)
    m0, m1, h = tiles(v, row, count)
    hs, m1s = turn(h, 64), turn(m1, 64)
    right = to_right(m0, m1, h, hs, m1s, lane, s)
    left = to_left(m0, m1, h, hs, m1s, lane, s)
    across = (m1, m0, hs)
    up = tiles(v, row - 1, count)
    down = tiles(v, row + 1, count)
    mid = (m0, m1, h)
    rows = pl.ds(row, count)
    out = []
    for t in range(3):
        near = e[0, t, rows, :] * up[t] + e[1, t, rows, :] * down[t]
        side = e[2, t, rows, :] * right[t] + e[3, t, rows, :] * left[t]
        out.append(
            (near + side) + (e[4, t, rows, :] * across[t] + (g[t, rows, :] - DAMPING * mid[t]))
        )
    return out, mid


def sweep(v, out, g, e, level, low, high):
    def body(row, count):
        delta, mid = change(v, g, e, level, row, count)
        for t in range(3):
            out[t, pl.ds(row, count), :] = mid[t] + delta[t]

    over(level, low, high, body)


def residual(v, out, g, e, level, low, high):
    def body(row, count):
        delta, _ = change(v, g, e, level, row, count)
        for t in range(3):
            out[t, pl.ds(row, count), :] = delta[t] * e[6, t, pl.ds(row, count), :]

    over(level, low, high, body)


def pair_sum(value, lane, s):
    both = value + turn(value, -s)
    return jnp.where(lane % (2 * s) < s, both, turn(both, s))


def even_odd(ref, index, row, count):
    first = ref[(*index, pl.ds(row, count, stride=2), slice(None))]
    second = ref[(*index, pl.ds(row + 1, count, stride=2), slice(None))]
    return first, second


def restrict(fine, g, e, level, low, high):
    s = 2 ** (level - 1)

    def body(row, count):
        lane = lanes_of(count)
        source = TOP[level - 1] + 2 * (row - TOP[level])
        for t in range(3):
            first, second = even_odd(fine, (t,), source, count)
            g[t, pl.ds(row, count), :] = pair_sum(first + second, lane, s) * e[5, t, pl.ds(row, count), :]

    over(level, low, high, body)


def prolong(coarse, fine, level, low, high):
    def body(row, count):
        target = TOP[level - 1] + 2 * (row - TOP[level])
        for t in range(3):
            value = coarse[t, pl.ds(row, count), :]
            for k in range(2):
                rows = pl.ds(target + k, count, stride=2)
                fine[t, rows, :] = fine[t, rows, :] + value

    over(level, low, high, body)


def coarsen(fine, coarse, level, low, high):
    s = 2 ** (level - 1)

    def body(row, count):
        lane = lanes_of(count)
        source = TOP[level - 1] + 2 * (row - TOP[level])
        rows = pl.ds(row, count)
        for t in range(3):
            first, second = even_odd(fine, (0, t), source, count)
            total = first + second
            coarse[0, t, rows, :] = jnp.where(lane % (2 * s) < s, turn(total, -s), total)
            second = fine[1, t, pl.ds(source + 1, count, stride=2), :]
            coarse[1, t, rows, :] = pair_sum(second, lane, s)
            for k in (2, 3):
                first, second = even_odd(fine, (k, t), source, count)
                coarse[k, t, rows, :] = pair_sum(first + second, lane, s)

    over(level, low, high, body)


def scale(faces, e, level, low, high):
    s = 2**level

    def body(row, count):
        lane = lanes_of(count)
        rows = pl.ds(row, count)
        east = tiles(faces.at[0], row, count)
        west = to_left(*east, turn(east[2], 64), turn(east[1], 64), lane, s)
        for t in range(3):
            south = faces[1, t, rows, :]
            north = faces[1, t, pl.ds(row - 1, count), :]
            across = faces[2, t, rows, :]
            diag = ((north + south) + (east[t] + west[t])) + (across + faces[3, t, rows, :])
            w = DAMPING / diag
            e[0, t, rows, :] = w * north
            e[1, t, rows, :] = w * south
            e[2, t, rows, :] = w * east[t]
            e[3, t, rows, :] = w * west[t]
            e[4, t, rows, :] = w * across
            e[5, t, rows, :] = w
            e[6, t, rows, :] = diag * (1.0 / DAMPING)

    over(level, low, high, body)


def harmonic(left, right):
    return 2.0 * left * right / (left + right)


def fine_faces(perm, faces, gx, gy, nx, ny, low, high):
    def body(row, count):
        lane = lanes_of(count)
        at = lax.broadcasted_iota(jnp.int32, (count, LANES), 0) + (row - TOP[0])
        m0, m1, h = tiles(perm, row, count)
        hs, m1s = turn(h, 64), turn(m1, 64)
        right = to_right(m0, m1, h, hs, m1s, lane, 1)
        below = tiles(perm, row + 1, count)
        wall = ((at == -1) & (gx == 0)) | ((at == ROWS - 1) & (gx == nx - 1))
        east = (lane == LANES - 1) & (gy == ny - 1)
        west = ((lane == LANES - 1) | (lane == 63)) & (gy == 0)
        own = (m0, m1, h)
        for t in range(3):
            edge = west if t == 2 else east
            faces[0, t, pl.ds(row, count), :] = jnp.where(edge, 0.0, harmonic(own[t], right[t]))
            faces[1, t, pl.ds(row, count), :] = jnp.where(wall, 0.0, harmonic(own[t], below[t]))
        between = VERTICAL * harmonic(m0, m1)
        faces[2, 0, pl.ds(row, count), :] = between
        faces[2, 1, pl.ds(row, count), :] = between
        faces[2, 2, pl.ds(row, count), :] = VERTICAL * harmonic(h, hs)

    over(0, low, high, body)


def vcycle(levels, spare, last):
    (e0, g0), (e1, g1), (e2, g2) = levels
    va, vb, r0, ua, ub, r1, wa, wb = spare
    sweep(va, vb, g0, e0, 0, -32, 96)
    residual(vb, r0, g0, e0, 0, -24, 88)
    restrict(r0, g1, e1, 1, -16, 48)
    sweep(g1, ub, g1, e1, 1, -16, 48)
    residual(ub, r1, g1, e1, 1, -16, 48)
    restrict(r1, g2, e2, 2, -8, 24)
    sweep(g2, wa, g2, e2, 2, -8, 24)
    sweep(wa, wb, g2, e2, 2, -8, 24)
    sweep(wb, wa, g2, e2, 2, -8, 24)
    prolong(wa, ub, 2, -4, 20)
    sweep(ub, ua, g1, e1, 1, -8, 40)
    sweep(ua, ub, g1, e1, 1, -8, 40)
    prolong(ub, vb, 1, -8, 40)
    sweep(vb, va, g0, e0, 0, -8, 72)
    sweep(va, last, g0, e0, 0, -8, 72)


def pack(m0, m1, to_west, to_east, index):
    lane = lanes_of(32)
    m1s = turn(m1, 64)
    outer = lane % 64 < 32
    for source, target, keep in (
        (jnp.where(lane < 64, m0, m1s), to_west, outer),
        (jnp.where(lane < 64, m1s, m0), to_east, jnp.logical_not(outer)),
    ):
        target[index] = jnp.where(keep[:16], source[:16], turn(source[16:], 32))


def unpack(from_west, from_east, target, source_index, row):
    outer = lanes_of(16) % 64 < 32
    west, east = from_west[source_index], from_east[source_index]
    target[pl.ds(row, 16), :] = jnp.where(outer, east, west)
    target[pl.ds(row + 16, 16), :] = turn(jnp.where(outer, west, east), -32)


def kernel(
    perm_log, facies, facies_scale, accumulation, previous, observed, well_cells, well_rates,
    pressure_out, adjoint_out, gradient_out,
    log_v, facies_v, observed_v, ext, ext2, to_west, to_east, from_west, from_east,
    to_west2, to_east2, from_west2, from_east2,
    f0, f1, f2, e0, e1, e2, g0, g1, g2, va, vb, r0, ua, ub, r1, wa, wb, pv, terms, total,
    load_sem, store_sem, send1, recv1, send2, recv2, send3, recv3,
):
    nx, ny, ns = lax.axis_size("gx"), lax.axis_size("gy"), lax.axis_size("scen")
    gx, gy, me = lax.axis_index("gx"), lax.axis_index("gy"), lax.axis_index("scen")
    north, south = lax.rem(gx + nx - 1, nx), lax.rem(gx + 1, nx)
    west, east = lax.rem(gy + ny - 1, ny), lax.rem(gy + 1, ny)
    around = [
        {"gx": north}, {"gx": south}, {"gy": west}, {"gy": east},
        {"gx": north, "gy": west}, {"gx": north, "gy": east},
        {"gx": south, "gy": west}, {"gx": south, "gy": east},
    ]
    peers = [{"scen": lax.rem(me + k, ns)} for k in range(1, ns)]

    own = pl.ds(TOP[0], ROWS)
    loads = [
        pltpu.make_async_copy(perm_log, log_v, load_sem.at[0]),
        pltpu.make_async_copy(facies, facies_v, load_sem.at[1]),
        pltpu.make_async_copy(accumulation, ext.at[1, 0:2, own, :], load_sem.at[2]),
        pltpu.make_async_copy(previous.at[0], ext.at[2, 0:2, own, :], load_sem.at[3]),
        pltpu.make_async_copy(observed.at[0], observed_v, load_sem.at[4]),
    ]
    for copy in loads:
        copy.start()
    barrier = pltpu.get_barrier_semaphore()
    for target in around + peers:
        pl.semaphore_signal(barrier, inc=1, device_id=target, device_id_type=MESH)

    for copy in loads[:4]:
        copy.wait()
    for layer in range(2):
        labels = facies_v[layer]
        factor = jnp.zeros((ROWS, LANES), jnp.float32)
        for label in range(FACIES):
            factor = jnp.where(labels == label, facies_scale[label], factor)
        ext[0, layer, own, :] = jnp.exp(log_v[layer]) * factor
    for field in range(3):
        for half in range(2):
            rows = pl.ds(TOP[0] + 32 * half, 32)
            pack(ext[field, 0, rows, :], ext[field, 1, rows, :], to_west, to_east, (field, pl.ds(16 * half, 16), slice(None)))
    pl.semaphore_wait(barrier, len(around) + len(peers))

    def exchange(block, w_out, e_out, w_in, e_in, send, recv):
        upper, lower = pl.ds(TOP[0], HALO), pl.ds(TOP[0] + ROWS - HALO, HALO)
        above, below = pl.ds(GUARD, HALO), pl.ds(TOP[0] + ROWS, HALO)
        first, second = pl.ds(0, 16), pl.ds(16, 16)
        lead = (slice(None),) * (len(w_out.shape) - 2)
        pairs = [
            (block.at[(*lead, slice(0, 2), upper)], block.at[(*lead, slice(0, 2), below)]),
            (block.at[(*lead, slice(0, 2), lower)], block.at[(*lead, slice(0, 2), above)]),
            (w_out, e_in.at[(*lead, pl.ds(16, 32))]),
            (e_out, w_in.at[(*lead, pl.ds(16, 32))]),
            (w_out.at[(*lead, first)], e_in.at[(*lead, pl.ds(48, 16))]),
            (e_out.at[(*lead, first)], w_in.at[(*lead, pl.ds(48, 16))]),
            (w_out.at[(*lead, second)], e_in.at[(*lead, pl.ds(0, 16))]),
            (e_out.at[(*lead, second)], w_in.at[(*lead, pl.ds(0, 16))]),
        ]
        copies = [
            pltpu.make_async_remote_copy(
                src_ref=source, dst_ref=target, send_sem=send.at[k], recv_sem=recv.at[k],
                device_id=around[k], device_id_type=MESH,
            )
            for k, (source, target) in enumerate(pairs)
        ]
        for k in (4, 5, 6, 7, 2, 3, 0, 1):
            copies[k].start()
        return copies

    copies1 = exchange(ext, to_west, to_east, from_west, from_east, send1, recv1)
    for copy in copies1:
        copy.wait_recv()
    for field in range(3):
        for block in range(4):
            unpack(from_west, from_east, ext.at[field, 2], (field, pl.ds(16 * block, 16), slice(None)), GUARD + 32 * block)

    perm, accu, start = ext.at[0], ext.at[1], ext.at[2]
    fine_faces(perm, f0, gx, gy, nx, ny, -32, 96)

    def keep_accumulation(row, count):
        for t in range(3):
            f0[3, t, pl.ds(row, count), :] = accu[t, pl.ds(row, count), :]

    over(0, -32, 96, keep_accumulation)
    coarsen(f0, f1, 1, -16, 48)
    coarsen(f1, f2, 2, -8, 24)
    scale(f0, e0, 0, -32, 96)
    scale(f1, e1, 1, -16, 48)
    scale(f2, e2, 2, -8, 24)

    plane, width = nx * ROWS * ny * LANES, ny * LANES

    def right_side(row, count):
        lane = lanes_of(count)
        at = lax.broadcasted_iota(jnp.int32, (count, LANES), 0) + (row - TOP[0] + gx * ROWS)
        flat = at * width + lane + gy * LANES
        middle = (lane >= 32) & (lane < 96)
        side = jnp.where(lane >= 64, lane - LANES, lane + LANES)
        side = jnp.where(middle, jnp.where(lane >= 64, lane + 64, lane - 64), side)
        flat_side = at * width + side + gy * LANES + jnp.where(middle, plane, 0)
        places = (flat, flat + plane, flat_side)
        for t in range(3):
            source = jnp.zeros((count, LANES), jnp.float32)
            for number in range(WELLS):
                source = source + jnp.where(places[t] == well_cells[0, number], well_rates[0, number], 0.0)
            rows = pl.ds(row, count)
            g0[t, rows, :] = e0[5, t, rows, :] * (accu[t, rows, :] * start[t, rows, :] + source)

    over(0, -32, 96, right_side)
    levels = ((e0, g0), (e1, g1), (e2, g2))
    spare = (va, vb, r0, ua, ub, r1, wa, wb)
    sweep(start, va, g0, e0, 0, -32, 96)
    vcycle(levels, spare, pv)

    loads[4].wait()
    for layer in range(2):
        ext2[layer, own, :] = pv[layer, own, :] - observed_v[layer]
    for half in range(2):
        rows = pl.ds(TOP[0] + 32 * half, 32)
        pack(ext2[0, rows, :], ext2[1, rows, :], to_west2, to_east2, (pl.ds(16 * half, 16), slice(None)))
    copies2 = exchange(ext2, to_west2, to_east2, from_west2, from_east2, send2, recv2)
    stores = [pltpu.make_async_copy(pv.at[0:2, own, :], pressure_out.at[0], store_sem.at[0])]
    stores[0].start()
    for copy in copies2:
        copy.wait_recv()
    for block in range(4):
        unpack(from_west2, from_east2, ext2.at[2], (pl.ds(16 * block, 16), slice(None)), GUARD + 32 * block)

    def adjoint_side(row, count):
        for t in range(3):
            rows = pl.ds(row, count)
            value = e0[5, t, rows, :] * ext2[t, rows, :]
            g0[t, rows, :] = value
            va[t, rows, :] = value

    over(0, -32, 96, adjoint_side)
    vcycle(levels, spare, vb)
    stores.append(pltpu.make_async_copy(vb.at[0:2, own, :], adjoint_out.at[0], store_sem.at[1]))
    stores[1].start()

    def gradient(row, count):
        lane = lanes_of(count)
        rows = pl.ds(row, count)
        before, after = pl.ds(row - 1, count), pl.ds(row + 1, count)
        p, a = tiles(pv, row, count), tiles(vb, row, count)
        pr = to_right(*p, turn(p[2], 64), turn(p[1], 64), lane, 1)
        ar = to_right(*a, turn(a[2], 64), turn(a[1], 64), lane, 1)
        ge = []
        for t in range(3):
            c = f0[0, t, rows, :]
            ge.append(c * c * (p[t] - pr[t]) * (a[t] - ar[t]))
        gw = to_left(*ge, turn(ge[2], 64), ge[1], lane, 1)
        c = f0[2, 0, rows, :]
        gv = c * c * (1.0 / VERTICAL) * (p[0] - p[1]) * (a[0] - a[1])
        for t in range(2):
            c = f0[1, t, rows, :]
            gs = c * c * (p[t] - pv[t, after, :]) * (a[t] - vb[t, after, :])
            c = f0[1, t, before, :]
            gn = c * c * (p[t] - pv[t, before, :]) * (a[t] - vb[t, before, :])
            total_faces = ((ge[t] + gw[t]) + (gs + gn)) + gv
            terms[me, t, pl.ds(row - TOP[0], count), :] = -0.5 * total_faces / perm[t, rows, :]

    copies3 = []
    for half in range(2):
        over(0, 32 * half, 32 * half + 32, gradient)
        part = terms.at[me, :, pl.ds(32 * half, 32), :]
        for k, target in enumerate(peers):
            copy = pltpu.make_async_remote_copy(
                src_ref=part, dst_ref=part, send_sem=send3.at[half, k], recv_sem=recv3.at[half, k],
                device_id=target, device_id_type=MESH,
            )
            copy.start()
            copies3.append(copy)
    for copy in copies3:
        copy.wait_recv()
    value = terms[0]
    for k in range(1, terms.shape[0]):
        value = value + terms[k]
    total[...] = value
    stores.append(pltpu.make_async_copy(total, gradient_out, store_sem.at[2]))
    stores[2].start()
    for copy in copies1 + copies2 + copies3:
        copy.wait_send()
    for copy in stores:
        copy.wait()


def shards(perm_log, facies, facies_scale, accumulation, previous, observed, well_cells, well_rates):
    ns = lax.axis_size("scen")
    f32 = jnp.float32
    block = (2, ROWS, LANES)
    anywhere = pl.BlockSpec(memory_space=pl.ANY)
    scalars = pl.BlockSpec(memory_space=pltpu.SMEM)

    def vmem(*shape):
        return pltpu.VMEM(shape, f32)

    level = [(3, HEIGHT[k], LANES) for k in range(3)]
    dma = pltpu.SemaphoreType.DMA
    scratch = [
        vmem(*block), pltpu.VMEM(block, jnp.int32), vmem(*block), vmem(3, *level[0]), vmem(*level[0]),
        vmem(3, 32, LANES), vmem(3, 32, LANES), vmem(3, 64, LANES), vmem(3, 64, LANES),
        vmem(32, LANES), vmem(32, LANES), vmem(64, LANES), vmem(64, LANES),
        *[vmem(4, *level[k]) for k in range(3)],
        *[vmem(7, *level[k]) for k in range(3)],
        *[vmem(*level[k]) for k in range(3)],
        *[vmem(*level[0]) for _ in range(3)],
        *[vmem(*level[1]) for _ in range(3)],
        *[vmem(*level[2]) for _ in range(2)],
        vmem(*level[0]), vmem(ns, *block), vmem(*block),
        dma((5,)), dma((3,)), dma((8,)), dma((8,)), dma((8,)), dma((8,)), dma((2, ns - 1)), dma((2, ns - 1)),
    ]
    return pl.pallas_call(
        kernel,
        out_shape=(
            jax.ShapeDtypeStruct((1, *block), f32),
            jax.ShapeDtypeStruct((1, *block), f32),
            jax.ShapeDtypeStruct(block, f32),
        ),
        in_specs=[anywhere, anywhere, scalars, anywhere, anywhere, anywhere, scalars, scalars],
        out_specs=(anywhere, anywhere, anywhere),
        scratch_shapes=scratch,
        compiler_params=pltpu.CompilerParams(
            collective_id=0, has_side_effects=True, vmem_limit_bytes=48 * 2**20
        ),
    )(perm_log, facies, facies_scale, accumulation, previous, observed, well_cells, well_rates)


def solution(mesh):
    return jax.shard_map(
        shards,
        mesh=mesh,
        in_specs=(
            P(None, "gx", "gy"),
            P(None, "gx", "gy"),
            P(),
            P(None, "gx", "gy"),
            P("scen", None, "gx", "gy"),
            P("scen", None, "gx", "gy"),
            P("scen", None),
            P("scen", None),
        ),
        out_specs=(P("scen", None, "gx", "gy"), P("scen", None, "gx", "gy"), P(None, "gx", "gy")),
        check_vma=False,
    )
```

time: 743 us -> 46.1 us (0.06); the launches traced: 733 us -> 45.7 us
  starting transfers between devices: 345 us -> 0 us
  waiting for transfers between devices: 159 us -> 0 us
  local copies, waits for them, and re-layouts: 146 us -> 8.04 us
  other arithmetic: 65.3 us -> 0 us
  Pallas kernels: 0 us -> 37 us
  between operations: 17.6 us -> 0.66 us
    ppermute x114 -> x0, starting transfers between devices: 345 us -> none  [the longest x62 199 us: passed_along(): lax.ppermute(value, axis, [(source, source + steps) for source in range(f...]
    ppermute x114 -> x0, waiting for transfers between devices: 110 us -> none  [the longest x23 54.9 us: extended(): lax.ppermute(lax.slice_in_dim(block, 0, width, axis=dim), axis, backward)]
    psum x1 -> x0, waiting for transfers between devices: 49.4 us -> none  [shards(): gradient = lax.psum(-local_terms, 'scen')]
    slice x87 -> x0, local copies, waits for them, and re-layouts: 45 us -> none  [the longest x2 25 us: coarsen(): quads[3, :, :, 1, :, 1]]
    pallas_call x0 -> x1, Pallas kernels: none -> 37 us  [shards(): pl.pallas_call(kernel, out_shape=(jax.ShapeDtypeStruct((1, *block), f32),...]
    unnamed x158 -> x19, local copies, waits for them, and re-layouts: 34.5 us -> 8.04 us
    squeeze x6 -> x0, local copies, waits for them, and re-layouts: 23.6 us -> none  [the longest x2 8.37 us: coarsen(): quads[6]]
    another operation x11 -> x0, local copies, waits for them, and re-layouts: 23.4 us -> none  [the longest x4 22.2 us: build_coeffs(): jnp.stack([harmonic(permeability, beside[0]), harmonic(permeability, besi...]
  transfers between devices with their start and end apart: 115 -> 0, of which waited for: 44 -> 0; matrix products, arithmetic and copies ran while one was open for 24% -> 0% of each run, Pallas kernels for 0% -> 0%
where the time goes in v1:
time: 46.1 us; the launch traced here: 45.7 us
  Pallas kernels  37 us (80%)
  local copies, waits for them, and re-layouts  8.04 us (17%)
  between operations  0.66 us (1%)
    pallas_call x1, Pallas kernels, shards(): pl.pallas_call(kernel, out_shape=(jax.ShapeDtypeStruct((1, *block), f32),...  37 us
    unnamed x19, local copies, waits for them, and re-layouts  8.04 us

profile of v1, /device:TPU:1, one launch (start us, length us, event | category | flops | bytes accessed | tf_op | source)
XLA Modules:
  0.0 45.7 jit_solution(2570194949708740827)
XLA Ops:
  0.6 0.0 copy-start
  0.6 0.8 %copy-done = f32[2,64,128]{2,1,0:T(8,128)S(1)} copy-done((f32[2,64,128]{2,1,0:T(8,128)S(1)}, f32[2,64,128]{2,1,0:T(8,128)}, u32[]{:S(2)}) %copy-start) | copy-done | bytes 65560
  1.5 0.0 copy-start.1
  1.5 0.8 %copy-done.1 = s32[2,64,128]{2,1,0:T(8,128)S(1)} copy-done((s32[2,64,128]{2,1,0:T(8,128)S(1)}, s32[2,64,128]{2,1,0:T(8,128)}, u32[]{:S(2)}) %copy-start.1) | copy-done | bytes 65560
  2.3 0.0 copy-start.2
  2.3 0.8 %copy-done.2 = f32[2,64,128]{2,1,0:T(8,128)S(1)} copy-done((f32[2,64,128]{2,1,0:T(8,128)S(1)}, f32[2,64,128]{2,1,0:T(8,128)}, u32[]{:S(2)}) %copy-start.2) | copy-done | bytes 65560
  3.2 0.0 copy-start.3
  3.2 0.8 %copy-done.3 = f32[1,2,64,128]{3,2,1,0:T(8,128)S(1)} copy-done((f32[1,2,64,128]{3,2,1,0:T(8,128)S(1)}, f32[1,2,64,128]{3,2,1,0:T(8,128)}, u32[]{:S(2)}) %copy-start.3) | copy-done | bytes 65560
  4.0 0.0 copy-start.4
  4.0 0.8 %copy-done.4 = f32[1,2,64,128]{3,2,1,0:T(8,128)S(1)} copy-done((f32[1,2,64,128]{3,2,1,0:T(8,128)S(1)}, f32[1,2,64,128]{3,2,1,0:T(8,128)}, u32[]{:S(2)}) %copy-start.4) | copy-done | bytes 65560
  4.8 0.0 copy-start.5
  4.8 0.7 %copy-done.5 = f32[4]{0:T(128)S(1)} copy-done((f32[4]{0:T(128)S(1)}, f32[4]{0:T(128)}, u32[]{:S(2)}) %copy-start.5) | copy-done | bytes 40
  5.5 0.0 copy-start.6
  5.5 0.7 %copy-done.6 = s32[1,5]{1,0:T(1,128)S(1)} copy-done((s32[1,5]{1,0:T(1,128)S(1)}, s32[1,5]{1,0:T(1,128)}, u32[]{:S(2)}) %copy-start.6) | copy-done | bytes 44
  6.1 0.0 copy-start.7
  6.1 0.7 %copy-done.7 = f32[1,5]{1,0:T(1,128)S(1)} copy-done((f32[1,5]{1,0:T(1,128)S(1)}, f32[1,5]{1,0:T(1,128)}, u32[]{:S(2)}) %copy-start.7) | copy-done | bytes 44
  6.8 37.0 %shard_map.103 = (f32[1,2,64,128]{3,2,1,0:T(8,128)S(1)}, f32[1,2,64,128]{3,2,1,0:T(8,128)S(1)}, f32[2,64,128]{2,1,0:T(8,128)S(1)}) custom-call(f32[2,64,128]{2,1,0:T(8,128)S(1)} %copy-done, s32[2,64,128]{2,1,0:T(8,128)S(1)} %copy-done.1, f32[4]{0:T(128)S(1)} %copy-done.5, f32[2,64,128]{2,1,0:T(8,128)S(1)} %copy-done.2, f32[1,2,64,128]{3,2,1,0:T(8,128)S(1)} %copy-done.3, ...), custom_call_target="tpu_custom_call" | custom-call | tf_op jit(solution)/shard_map/pallas_call | solution.py:462
  43.8 0.6 %copy.14 = f32[1,2,64,128]{3,2,1,0:T(8,128)} copy(f32[1,2,64,128]{3,2,1,0:T(8,128)S(1)} %get-tuple-element.6) | data formatting | bytes 131072
  44.5 0.6 %copy.15 = f32[1,2,64,128]{3,2,1,0:T(8,128)} copy(f32[1,2,64,128]{3,2,1,0:T(8,128)S(1)} %get-tuple-element.7) | data formatting | bytes 131072
  45.1 0.6 %copy.16 = f32[2,64,128]{2,1,0:T(8,128)} copy(f32[2,64,128]{2,1,0:T(8,128)S(1)} %get-tuple-element.8) | data formatting | bytes 131072
Async XLA Ops:
  0.6 0.8 %copy-start = (f32[2,64,128]{2,1,0:T(8,128)S(1)}, f32[2,64,128]{2,1,0:T(8,128)}, u32[]{:S(2)}) copy-start(f32[2,64,128]{2,1,0:T(8,128)} %perm_log.1) | copy-start | bytes 196612
  1.5 0.8 %copy-start.1 = (s32[2,64,128]{2,1,0:T(8,128)S(1)}, s32[2,64,128]{2,1,0:T(8,128)}, u32[]{:S(2)}) copy-start(s32[2,64,128]{2,1,0:T(8,128)} %facies.1) | copy-start | bytes 196612
  2.3 0.8 %copy-start.2 = (f32[2,64,128]{2,1,0:T(8,128)S(1)}, f32[2,64,128]{2,1,0:T(8,128)}, u32[]{:S(2)}) copy-start(f32[2,64,128]{2,1,0:T(8,128)} %accumulation.1) | copy-start | bytes 196612
  3.2 0.8 %copy-start.3 = (f32[1,2,64,128]{3,2,1,0:T(8,128)S(1)}, f32[1,2,64,128]{3,2,1,0:T(8,128)}, u32[]{:S(2)}) copy-start(f32[1,2,64,128]{3,2,1,0:T(8,128)} %previous.1) | copy-start | bytes 196612
  4.0 0.8 %copy-start.4 = (f32[1,2,64,128]{3,2,1,0:T(8,128)S(1)}, f32[1,2,64,128]{3,2,1,0:T(8,128)}, u32[]{:S(2)}) copy-start(f32[1,2,64,128]{3,2,1,0:T(8,128)} %observed.1) | copy-start | bytes 196612
  4.8 0.7 %copy-start.5 = (f32[4]{0:T(128)S(1)}, f32[4]{0:T(128)}, u32[]{:S(2)}) copy-start(f32[4]{0:T(128)} %facies_scale.1) | copy-start | bytes 52
  5.5 0.7 %copy-start.6 = (s32[1,5]{1,0:T(1,128)S(1)}, s32[1,5]{1,0:T(1,128)}, u32[]{:S(2)}) copy-start(s32[1,5]{1,0:T(1,128)} %well_cells.1) | copy-start | bytes 64
  6.1 0.7 %copy-start.7 = (f32[1,5]{1,0:T(1,128)S(1)}, f32[1,5]{1,0:T(1,128)}, u32[]{:S(2)}) copy-start(f32[1,5]{1,0:T(1,128)} %well_rates.1) | copy-start | bytes 64

commit v2 on v1

--- a/solution.py
+++ b/solution.py
@@ -15,11 +15,12 @@
 LANES = 128
 HALO = 32
 GUARD = 8
+VMEM = 62 * 2**20
 MESH = pl.DeviceIdType.MESH
 
 TOP = (GUARD + HALO, GUARD + HALO // 2, GUARD + HALO // 4)
 HEIGHT = tuple(ROWS // 2**k + 2 * TOP[k] for k in range(3))
-CHUNK = 16
+CHUNK = 128
 
 
 def over(level, low, high, body, step=CHUNK):
@@ -244,12 +245,12 @@
 
 
 def kernel(
-    perm_log, facies, facies_scale, accumulation, previous, observed, well_cells, well_rates,
+    perm_log, facies, scale_in, accumulation, previous, observed, cells_in, rates_in,
     pressure_out, adjoint_out, gradient_out,
-    log_v, facies_v, observed_v, ext, ext2, to_west, to_east, from_west, from_east,
+    facies_scale, well_cells, well_rates, log_v, facies_v, observed_v, ext, ext2, to_west, to_east, from_west, from_east,
     to_west2, to_east2, from_west2, from_east2,
-    f0, f1, f2, e0, e1, e2, g0, g1, g2, va, vb, r0, ua, ub, r1, wa, wb, pv, terms, total,
-    load_sem, store_sem, send1, recv1, send2, recv2, send3, recv3,
+    f0, f1, f2, e0, e1, e2, g0, g1, g2, va, vb, r0, ua, ub, r1, wa, wb, pv, terms,
+    load_sem, send1, recv1, send2, recv2, send3, recv3,
 ):
     nx, ny, ns = lax.axis_size("gx"), lax.axis_size("gy"), lax.axis_size("scen")
     gx, gy, me = lax.axis_index("gx"), lax.axis_index("gy"), lax.axis_index("scen")
@@ -268,7 +269,10 @@
         pltpu.make_async_copy(facies, facies_v, load_sem.at[1]),
         pltpu.make_async_copy(accumulation, ext.at[1, 0:2, own, :], load_sem.at[2]),
         pltpu.make_async_copy(previous.at[0], ext.at[2, 0:2, own, :], load_sem.at[3]),
-        pltpu.make_async_copy(observed.at[0], observed_v, load_sem.at[4]),
+        pltpu.make_async_copy(scale_in, facies_scale, load_sem.at[4]),
+        pltpu.make_async_copy(cells_in, well_cells, load_sem.at[5]),
+        pltpu.make_async_copy(rates_in, well_rates, load_sem.at[6]),
+        pltpu.make_async_copy(observed.at[0], observed_v, load_sem.at[7]),
     ]
     for copy in loads:
         copy.start()
@@ -276,7 +280,7 @@
     for target in around + peers:
         pl.semaphore_signal(barrier, inc=1, device_id=target, device_id_type=MESH)
 
-    for copy in loads[:4]:
+    for copy in loads[:7]:
         copy.wait()
     for layer in range(2):
         labels = facies_v[layer]
@@ -361,15 +365,14 @@
     sweep(start, va, g0, e0, 0, -32, 96)
     vcycle(levels, spare, pv)
 
-    loads[4].wait()
+    loads[7].wait()
     for layer in range(2):
         ext2[layer, own, :] = pv[layer, own, :] - observed_v[layer]
     for half in range(2):
         rows = pl.ds(TOP[0] + 32 * half, 32)
         pack(ext2[0, rows, :], ext2[1, rows, :], to_west2, to_east2, (pl.ds(16 * half, 16), slice(None)))
     copies2 = exchange(ext2, to_west2, to_east2, from_west2, from_east2, send2, recv2)
-    stores = [pltpu.make_async_copy(pv.at[0:2, own, :], pressure_out.at[0], store_sem.at[0])]
-    stores[0].start()
+    pressure_out[0] = pv[0:2, own, :]
     for copy in copies2:
         copy.wait_recv()
     for block in range(4):
@@ -384,8 +387,7 @@
 
     over(0, -32, 96, adjoint_side)
     vcycle(levels, spare, vb)
-    stores.append(pltpu.make_async_copy(vb.at[0:2, own, :], adjoint_out.at[0], store_sem.at[1]))
-    stores[1].start()
+    adjoint_out[0] = vb[0:2, own, :]
 
     def gradient(row, count):
         lane = lanes_of(count)
@@ -425,12 +427,17 @@
     value = terms[0]
     for k in range(1, terms.shape[0]):
         value = value + terms[k]
-    total[...] = value
-    stores.append(pltpu.make_async_copy(total, gradient_out, store_sem.at[2]))
-    stores[2].start()
+    gradient_out[...] = value
     for copy in copies1 + copies2 + copies3:
         copy.wait_send()
-    for copy in stores:
+
+
+def store(*refs):
+    sem = refs[-1]
+    copies = [pltpu.make_async_copy(refs[k], refs[k + 3], sem.at[k]) for k in range(3)]
+    for copy in copies:
+        copy.start()
+    for copy in copies:
         copy.wait()
 
 
@@ -439,7 +446,6 @@
     f32 = jnp.float32
     block = (2, ROWS, LANES)
     anywhere = pl.BlockSpec(memory_space=pl.ANY)
-    scalars = pl.BlockSpec(memory_space=pltpu.SMEM)
 
     def vmem(*shape):
         return pltpu.VMEM(shape, f32)
@@ -447,6 +453,7 @@
     level = [(3, HEIGHT[k], LANES) for k in range(3)]
     dma = pltpu.SemaphoreType.DMA
     scratch = [
+        pltpu.SMEM((FACIES,), f32), pltpu.SMEM((1, WELLS), jnp.int32), pltpu.SMEM((1, WELLS), f32),
         vmem(*block), pltpu.VMEM(block, jnp.int32), vmem(*block), vmem(3, *level[0]), vmem(*level[0]),
         vmem(3, 32, LANES), vmem(3, 32, LANES), vmem(3, 64, LANES), vmem(3, 64, LANES),
         vmem(32, LANES), vmem(32, LANES), vmem(64, LANES), vmem(64, LANES),
@@ -456,23 +463,28 @@
         *[vmem(*level[0]) for _ in range(3)],
         *[vmem(*level[1]) for _ in range(3)],
         *[vmem(*level[2]) for _ in range(2)],
-        vmem(*level[0]), vmem(ns, *block), vmem(*block),
-        dma((5,)), dma((3,)), dma((8,)), dma((8,)), dma((8,)), dma((8,)), dma((2, ns - 1)), dma((2, ns - 1)),
+        vmem(*level[0]), vmem(ns, *block),
+        dma((8,)), dma((8,)), dma((8,)), dma((8,)), dma((8,)), dma((2, ns - 1)), dma((2, ns - 1)),
     ]
-    return pl.pallas_call(
+    shapes = ((1, *block), (1, *block), block)
+    results = pl.pallas_call(
         kernel,
-        out_shape=(
-            jax.ShapeDtypeStruct((1, *block), f32),
-            jax.ShapeDtypeStruct((1, *block), f32),
-            jax.ShapeDtypeStruct(block, f32),
-        ),
-        in_specs=[anywhere, anywhere, scalars, anywhere, anywhere, anywhere, scalars, scalars],
-        out_specs=(anywhere, anywhere, anywhere),
+        out_shape=tuple(vmem(*shape) for shape in shapes),
+        in_specs=[anywhere] * 8,
+        out_specs=(pl.BlockSpec(memory_space=pltpu.VMEM),) * 3,
         scratch_shapes=scratch,
         compiler_params=pltpu.CompilerParams(
-            collective_id=0, has_side_effects=True, vmem_limit_bytes=48 * 2**20
+            collective_id=0, has_side_effects=True, vmem_limit_bytes=VMEM
         ),
     )(perm_log, facies, facies_scale, accumulation, previous, observed, well_cells, well_rates)
+    return pl.pallas_call(
+        store,
+        out_shape=tuple(jax.ShapeDtypeStruct(shape, f32) for shape in shapes),
+        in_specs=[anywhere] * 3,
+        out_specs=(anywhere,) * 3,
+        scratch_shapes=[dma((3,))],
+        compiler_params=pltpu.CompilerParams(vmem_limit_bytes=2**20),
+    )(*results)
 
 
 def solution(mesh):

time: 46.1 us -> 35.2 us (0.76)
  local copies, waits for them, and re-layouts: 8.04 us -> 0 us
  Pallas kernels: 37 us -> 34.4 us
    unnamed x19 -> x0, local copies, waits for them, and re-layouts: 8.04 us -> none
    pallas_call x1 -> x2, Pallas kernels: 37 us -> 34.4 us  [the longest x1 33.7 us: shards(): pl.pallas_call(kernel, out_shape=tuple((vmem(*shape) for shape in shapes)...]
where the time goes in v2:
time: 35.2 us; the launch traced here: 35.1 us
  Pallas kernels  34.4 us (98%)
  between operations  0.64 us (2%)
    pallas_call x1, Pallas kernels, shards(): pl.pallas_call(kernel, out_shape=tuple((vmem(*shape) for shape in shapes)...  33.7 us

profile of v2, /device:TPU:1, one launch (start us, length us, event | category | flops | bytes accessed | tf_op | source)
XLA Modules:
  0.0 35.1 jit_solution(7225610929290328384)
XLA Ops:
  0.6 33.7 %shard_map.103 = (f32[1,2,64,128]{3,2,1,0:T(8,128)S(1)}, f32[1,2,64,128]{3,2,1,0:T(8,128)S(1)}, f32[2,64,128]{2,1,0:T(8,128)S(1)}) custom-call(f32[2,64,128]{2,1,0:T(8,128)} %perm_log.1, s32[2,64,128]{2,1,0:T(8,128)} %facies.1, f32[4]{0:T(128)} %scale_in.1, f32[2,64,128]{2,1,0:T(8,128)} %accumulation.1, f32[1,2,64,128]{3,2,1,0:T(8,128)} %previous.1, ...), custom_call_target="tpu_custom_call" | custom-call | tf_op jit(solution)/shard_map/pallas_call | solution.py:470
  34.4 0.7 %shard_map.104 = (f32[1,2,64,128]{3,2,1,0:T(8,128)}, f32[1,2,64,128]{3,2,1,0:T(8,128)}, f32[2,64,128]{2,1,0:T(8,128)}) custom-call(f32[1,2,64,128]{3,2,1,0:T(8,128)S(1)} %get-tuple-element.6.refs_0_, f32[1,2,64,128]{3,2,1,0:T(8,128)S(1)} %get-tuple-element.7.refs_1_, f32[2,64,128]{2,1,0:T(8,128)S(1)} %get-tuple-element.8.refs_2_), custom_call_target="tpu_custom_call" | custom-call | tf_op jit(solution)/shard_map/pallas_call | solution.py:480

commit v3 on v2

--- a/solution.py
+++ b/solution.py
@@ -1,5 +1,3 @@
-from functools import partial
-
 import jax
 import jax.numpy as jnp
 from jax import lax
@@ -20,7 +18,8 @@
 
 TOP = (GUARD + HALO, GUARD + HALO // 2, GUARD + HALO // 4)
 HEIGHT = tuple(ROWS // 2**k + 2 * TOP[k] for k in range(3))
-CHUNK = 128
+CHUNK = 8
+TILES = 4
 
 
 def over(level, low, high, body, step=CHUNK):
@@ -37,44 +36,34 @@
     return pltpu.roll(value, shift % LANES, 1)
 
 
-def to_right(m0, m1, h, hs, m1s, lane, s):
-    return (
-        turn(jnp.where(lane < s, h, m0), -s),
-        turn(jnp.where(lane < s, hs, m1), -s),
-        turn(jnp.where(lane < s, m0, jnp.where((lane >= 64) & (lane < 64 + s), m1s, h)), -s),
-    )
-
-
-def to_left(m0, m1, h, hs, m1s, lane, s):
-    return (
-        turn(jnp.where(lane >= LANES - s, h, m0), s),
-        turn(jnp.where(lane >= LANES - s, hs, m1), s),
-        turn(jnp.where(lane >= LANES - s, m0, jnp.where((lane >= 64 - s) & (lane < 64), m1s, h)), s),
-    )
+def to_right(values, lane, s):
+    wrapped = lane < s
+    return [turn(jnp.where(wrapped, values[t ^ 2], values[t]), -s) for t in range(TILES)]
+
+
+def to_left(values, lane, s):
+    wrapped = lane >= LANES - s
+    return [turn(jnp.where(wrapped, values[t ^ 2], values[t]), s) for t in range(TILES)]
 
 
 def tiles(ref, row, count):
-    return tuple(ref[t, pl.ds(row, count), :] for t in range(3))
+    return [ref[t, pl.ds(row, count), :] for t in range(TILES)]
 
 
 def change(v, g, e, level, row, count):
     s = 2**level
     lane = lanes_of(count)
-    m0, m1, h = tiles(v, row, count)
-    hs, m1s = turn(h, 64), turn(m1, 64)
-    right = to_right(m0, m1, h, hs, m1s, lane, s)
-    left = to_left(m0, m1, h, hs, m1s, lane, s)
-    across = (m1, m0, hs)
+    mid = tiles(v, row, count)
+    right, left = to_right(mid, lane, s), to_left(mid, lane, s)
     up = tiles(v, row - 1, count)
     down = tiles(v, row + 1, count)
-    mid = (m0, m1, h)
     rows = pl.ds(row, count)
     out = []
-    for t in range(3):
+    for t in range(TILES):
         near = e[0, t, rows, :] * up[t] + e[1, t, rows, :] * down[t]
         side = e[2, t, rows, :] * right[t] + e[3, t, rows, :] * left[t]
         out.append(
-            (near + side) + (e[4, t, rows, :] * across[t] + (g[t, rows, :] - DAMPING * mid[t]))
+            (near + side) + (e[4, t, rows, :] * mid[t ^ 1] + (g[t, rows, :] - DAMPING * mid[t]))
         )
     return out, mid
 
@@ -82,7 +71,7 @@
 def sweep(v, out, g, e, level, low, high):
     def body(row, count):
         delta, mid = change(v, g, e, level, row, count)
-        for t in range(3):
+        for t in range(TILES):
             out[t, pl.ds(row, count), :] = mid[t] + delta[t]
 
     over(level, low, high, body)
@@ -91,15 +80,14 @@
 def residual(v, out, g, e, level, low, high):
     def body(row, count):
         delta, _ = change(v, g, e, level, row, count)
-        for t in range(3):
+        for t in range(TILES):
             out[t, pl.ds(row, count), :] = delta[t] * e[6, t, pl.ds(row, count), :]
 
     over(level, low, high, body)
 
 
 def pair_sum(value, lane, s):
-    both = value + turn(value, -s)
-    return jnp.where(lane % (2 * s) < s, both, turn(both, s))
+    return value + jnp.where(lane % (2 * s) < s, turn(value, -s), turn(value, s))
 
 
 def even_odd(ref, index, row, count):
@@ -114,7 +102,7 @@
     def body(row, count):
         lane = lanes_of(count)
         source = TOP[level - 1] + 2 * (row - TOP[level])
-        for t in range(3):
+        for t in range(TILES):
             first, second = even_odd(fine, (t,), source, count)
             g[t, pl.ds(row, count), :] = pair_sum(first + second, lane, s) * e[5, t, pl.ds(row, count), :]
 
@@ -124,7 +112,7 @@
 def prolong(coarse, fine, level, low, high):
     def body(row, count):
         target = TOP[level - 1] + 2 * (row - TOP[level])
-        for t in range(3):
+        for t in range(TILES):
             value = coarse[t, pl.ds(row, count), :]
             for k in range(2):
                 rows = pl.ds(target + k, count, stride=2)
@@ -133,22 +121,21 @@
     over(level, low, high, body)
 
 
-def coarsen(fine, coarse, level, low, high):
+def coarsen(fine, coarse, level, low, high, members):
     s = 2 ** (level - 1)
 
     def body(row, count):
         lane = lanes_of(count)
         source = TOP[level - 1] + 2 * (row - TOP[level])
         rows = pl.ds(row, count)
-        for t in range(3):
-            first, second = even_odd(fine, (0, t), source, count)
-            total = first + second
-            coarse[0, t, rows, :] = jnp.where(lane % (2 * s) < s, turn(total, -s), total)
-            second = fine[1, t, pl.ds(source + 1, count, stride=2), :]
-            coarse[1, t, rows, :] = pair_sum(second, lane, s)
-            for k in (2, 3):
+        for k in members:
+            for t in range(TILES):
                 first, second = even_odd(fine, (k, t), source, count)
-                coarse[k, t, rows, :] = pair_sum(first + second, lane, s)
+                if k == 0:
+                    total = first + second
+                    coarse[k, t, rows, :] = jnp.where(lane % (2 * s) < s, turn(total, -s), total)
+                else:
+                    coarse[k, t, rows, :] = pair_sum(second if k == 1 else first + second, lane, s)
 
     over(level, low, high, body)
 
@@ -160,8 +147,8 @@
         lane = lanes_of(count)
         rows = pl.ds(row, count)
         east = tiles(faces.at[0], row, count)
-        west = to_left(*east, turn(east[2], 64), turn(east[1], 64), lane, s)
-        for t in range(3):
+        west = to_left(east, lane, s)
+        for t in range(TILES):
             south = faces[1, t, rows, :]
             north = faces[1, t, pl.ds(row - 1, count), :]
             across = faces[2, t, rows, :]
@@ -186,22 +173,20 @@
     def body(row, count):
         lane = lanes_of(count)
         at = lax.broadcasted_iota(jnp.int32, (count, LANES), 0) + (row - TOP[0])
-        m0, m1, h = tiles(perm, row, count)
-        hs, m1s = turn(h, 64), turn(m1, 64)
-        right = to_right(m0, m1, h, hs, m1s, lane, 1)
+        own = tiles(perm, row, count)
+        right = to_right(own, lane, 1)
         below = tiles(perm, row + 1, count)
         wall = ((at == -1) & (gx == 0)) | ((at == ROWS - 1) & (gx == nx - 1))
-        east = (lane == LANES - 1) & (gy == ny - 1)
-        west = ((lane == LANES - 1) | (lane == 63)) & (gy == 0)
-        own = (m0, m1, h)
-        for t in range(3):
-            edge = west if t == 2 else east
-            faces[0, t, pl.ds(row, count), :] = jnp.where(edge, 0.0, harmonic(own[t], right[t]))
-            faces[1, t, pl.ds(row, count), :] = jnp.where(wall, 0.0, harmonic(own[t], below[t]))
-        between = VERTICAL * harmonic(m0, m1)
-        faces[2, 0, pl.ds(row, count), :] = between
-        faces[2, 1, pl.ds(row, count), :] = between
-        faces[2, 2, pl.ds(row, count), :] = VERTICAL * harmonic(h, hs)
+        last = lane == LANES - 1
+        edges = (last & (gy == ny - 1), last & (gy == 0))
+        rows = pl.ds(row, count)
+        for t in range(TILES):
+            faces[0, t, rows, :] = jnp.where(edges[t // 2], 0.0, harmonic(own[t], right[t]))
+            faces[1, t, rows, :] = jnp.where(wall, 0.0, harmonic(own[t], below[t]))
+        for t in (0, 2):
+            between = VERTICAL * harmonic(own[t], own[t + 1])
+            faces[2, t, rows, :] = between
+            faces[2, t + 1, rows, :] = between
 
     over(0, low, high, body)
 
@@ -227,21 +212,26 @@
 
 
 def pack(m0, m1, to_west, to_east, index):
-    lane = lanes_of(32)
-    m1s = turn(m1, 64)
+    lane = lanes_of(16)
     outer = lane % 64 < 32
-    for source, target, keep in (
-        (jnp.where(lane < 64, m0, m1s), to_west, outer),
-        (jnp.where(lane < 64, m1s, m0), to_east, jnp.logical_not(outer)),
-    ):
-        target[index] = jnp.where(keep[:16], source[:16], turn(source[16:], 32))
-
-
-def unpack(from_west, from_east, target, source_index, row):
+    first = lane < 64
+    turned = (lane >= 32) & (lane < 96)
+    upper = m0[:16], turn(m1[:16], 64)
+    lower = turn(m0[16:], 32), turn(m1[16:], 96)
+    for k, target in enumerate((to_west, to_east)):
+        a = jnp.where(first, upper[k], upper[1 - k])
+        b = jnp.where(turned, lower[k], lower[1 - k])
+        target[index] = jnp.where(outer, a, b) if k == 0 else jnp.where(outer, b, a)
+
+
+def unpack(from_west, from_east, block, index, row):
     outer = lanes_of(16) % 64 < 32
-    west, east = from_west[source_index], from_east[source_index]
-    target[pl.ds(row, 16), :] = jnp.where(outer, east, west)
-    target[pl.ds(row + 16, 16), :] = turn(jnp.where(outer, west, east), -32)
+    west, east = from_west[index], from_east[index]
+    upper, lower = jnp.where(outer, east, west), jnp.where(outer, west, east)
+    block[2, pl.ds(row, 16), :] = upper
+    block[3, pl.ds(row, 16), :] = turn(upper, 64)
+    block[2, pl.ds(row + 16, 16), :] = turn(lower, -32)
+    block[3, pl.ds(row + 16, 16), :] = turn(lower, 32)
 
 
 def kernel(
@@ -249,8 +239,8 @@
     pressure_out, adjoint_out, gradient_out,
     facies_scale, well_cells, well_rates, log_v, facies_v, observed_v, ext, ext2, to_west, to_east, from_west, from_east,
     to_west2, to_east2, from_west2, from_east2,
-    f0, f1, f2, e0, e1, e2, g0, g1, g2, va, vb, r0, ua, ub, r1, wa, wb, pv, terms,
-    load_sem, send1, recv1, send2, recv2, send3, recv3,
+    f0, f1, f2, e0, e1, e2, g0, g1, g2, va, vb, r0, ua, ub, r1, wa, wb, pv, q, terms,
+    load_sem, send0, recv0, send1, recv1, send2, recv2, send3, recv3,
 ):
     nx, ny, ns = lax.axis_size("gx"), lax.axis_size("gy"), lax.axis_size("scen")
     gx, gy, me = lax.axis_index("gx"), lax.axis_index("gy"), lax.axis_index("scen")
@@ -261,7 +251,7 @@
         {"gx": north, "gy": west}, {"gx": north, "gy": east},
         {"gx": south, "gy": west}, {"gx": south, "gy": east},
     ]
-    peers = [{"scen": lax.rem(me + k, ns)} for k in range(1, ns)]
+    peers = [{"scen": lax.rem(me + k, ns)} for k in sorted(range(1, ns), key=lambda k: -min(k, ns - k))]
 
     own = pl.ds(TOP[0], ROWS)
     loads = [
@@ -320,46 +310,60 @@
             copies[k].start()
         return copies
 
-    copies1 = exchange(ext, to_west, to_east, from_west, from_east, send1, recv1)
-    for copy in copies1:
-        copy.wait_recv()
-    for field in range(3):
-        for block in range(4):
-            unpack(from_west, from_east, ext.at[field, 2], (field, pl.ds(16 * block, 16), slice(None)), GUARD + 32 * block)
-
+    first, rest = pl.ds(0, 1), pl.ds(1, 2)
+    copies0, copies1 = [
+        exchange(*[ref.at[part] for ref in (ext, to_west, to_east, from_west, from_east)], send, recv)
+        for part, send, recv in ((first, send0, recv0), (rest, send1, recv1))
+    ]
+    plane, width = nx * ROWS * ny * LANES, ny * LANES
+
+    def sources(row, count):
+        lane = lanes_of(count)
+        at = lax.broadcasted_iota(jnp.int32, (count, LANES), 0) + (row - TOP[0] + gx * ROWS)
+        flat = at * width + lane + gy * LANES
+        side = flat + jnp.where(lane >= 64, -LANES, LANES)
+        for t, place in enumerate((flat, flat + plane, side, side + plane)):
+            source = jnp.zeros((count, LANES), jnp.float32)
+            for number in range(WELLS):
+                source = source + jnp.where(place == well_cells[0, number], well_rates[0, number], 0.0)
+            g0[t, pl.ds(row, count), :] = source
+
+    over(0, -32, 96, sources)
+
+    def receive(copies, fields):
+        for copy in copies:
+            copy.wait_recv()
+        for field in fields:
+            for block in range(4):
+                unpack(from_west, from_east, ext.at[field], (field, pl.ds(16 * block, 16), slice(None)), GUARD + 32 * block)
+
+    receive(copies0, (0,))
     perm, accu, start = ext.at[0], ext.at[1], ext.at[2]
     fine_faces(perm, f0, gx, gy, nx, ny, -32, 96)
-
-    def keep_accumulation(row, count):
-        for t in range(3):
-            f0[3, t, pl.ds(row, count), :] = accu[t, pl.ds(row, count), :]
-
-    over(0, -32, 96, keep_accumulation)
-    coarsen(f0, f1, 1, -16, 48)
-    coarsen(f1, f2, 2, -8, 24)
+    coarsen(f0, f1, 1, -16, 48, (0, 1, 2))
+    coarsen(f1, f2, 2, -8, 24, (0, 1, 2))
+    receive(copies1, (1, 2))
+
+    def right_side(row, count):
+        rows = pl.ds(row, count)
+        for t in range(TILES):
+            value = accu[t, rows, :]
+            f0[3, t, rows, :] = value
+            g0[t, rows, :] = g0[t, rows, :] + value * start[t, rows, :]
+
+    over(0, -32, 96, right_side)
     scale(f0, e0, 0, -32, 96)
+
+    def weigh(row, count):
+        rows = pl.ds(row, count)
+        for t in range(TILES):
+            g0[t, rows, :] = g0[t, rows, :] * e0[5, t, rows, :]
+
+    over(0, -32, 96, weigh)
+    coarsen(f0, f1, 1, -16, 48, (3,))
+    coarsen(f1, f2, 2, -8, 24, (3,))
     scale(f1, e1, 1, -16, 48)
     scale(f2, e2, 2, -8, 24)
-
-    plane, width = nx * ROWS * ny * LANES, ny * LANES
-
-    def right_side(row, count):
-        lane = lanes_of(count)
-        at = lax.broadcasted_iota(jnp.int32, (count, LANES), 0) + (row - TOP[0] + gx * ROWS)
-        flat = at * width + lane + gy * LANES
-        middle = (lane >= 32) & (lane < 96)
-        side = jnp.where(lane >= 64, lane - LANES, lane + LANES)
-        side = jnp.where(middle, jnp.where(lane >= 64, lane + 64, lane - 64), side)
-        flat_side = at * width + side + gy * LANES + jnp.where(middle, plane, 0)
-        places = (flat, flat + plane, flat_side)
-        for t in range(3):
-            source = jnp.zeros((count, LANES), jnp.float32)
-            for number in range(WELLS):
-                source = source + jnp.where(places[t] == well_cells[0, number], well_rates[0, number], 0.0)
-            rows = pl.ds(row, count)
-            g0[t, rows, :] = e0[5, t, rows, :] * (accu[t, rows, :] * start[t, rows, :] + source)
-
-    over(0, -32, 96, right_side)
     levels = ((e0, g0), (e1, g1), (e2, g2))
     spare = (va, vb, r0, ua, ub, r1, wa, wb)
     sweep(start, va, g0, e0, 0, -32, 96)
@@ -373,13 +377,32 @@
         pack(ext2[0, rows, :], ext2[1, rows, :], to_west2, to_east2, (pl.ds(16 * half, 16), slice(None)))
     copies2 = exchange(ext2, to_west2, to_east2, from_west2, from_east2, send2, recv2)
     pressure_out[0] = pv[0:2, own, :]
+
+    def gradient_weights(row, count):
+        lane = lanes_of(count)
+        rows, before, after = pl.ds(row, count), pl.ds(row - 1, count), pl.ds(row + 1, count)
+        p = tiles(pv, row, count)
+        right, left = to_right(p, lane, 1), to_left(p, lane, 1)
+        east = tiles(f0.at[0], row, count)
+        west = to_left(east, lane, 1)
+        for t in range(2):
+            factor = -0.5 / perm[t, rows, :]
+            south, north, across = f0[1, t, rows, :], f0[1, t, before, :], f0[2, t, rows, :]
+            sides = (
+                (north, pv[t, before, :], 1.0), (south, pv[t, after, :], 1.0), (east[t], right[t], 1.0),
+                (west[t], left[t], 1.0), (across, p[t ^ 1], 1.0 / VERTICAL),
+            )
+            for k, (face, value, weight) in enumerate(sides):
+                q[k, t, pl.ds(row - TOP[0], count), :] = factor * weight * (face * face) * (p[t] - value)
+
+    over(0, 0, ROWS, gradient_weights)
     for copy in copies2:
         copy.wait_recv()
     for block in range(4):
-        unpack(from_west2, from_east2, ext2.at[2], (pl.ds(16 * block, 16), slice(None)), GUARD + 32 * block)
+        unpack(from_west2, from_east2, ext2, (pl.ds(16 * block, 16), slice(None)), GUARD + 32 * block)
 
     def adjoint_side(row, count):
-        for t in range(3):
+        for t in range(TILES):
             rows = pl.ds(row, count)
             value = e0[5, t, rows, :] * ext2[t, rows, :]
             g0[t, rows, :] = value
@@ -391,25 +414,14 @@
 
     def gradient(row, count):
         lane = lanes_of(count)
-        rows = pl.ds(row, count)
         before, after = pl.ds(row - 1, count), pl.ds(row + 1, count)
-        p, a = tiles(pv, row, count), tiles(vb, row, count)
-        pr = to_right(*p, turn(p[2], 64), turn(p[1], 64), lane, 1)
-        ar = to_right(*a, turn(a[2], 64), turn(a[1], 64), lane, 1)
-        ge = []
-        for t in range(3):
-            c = f0[0, t, rows, :]
-            ge.append(c * c * (p[t] - pr[t]) * (a[t] - ar[t]))
-        gw = to_left(*ge, turn(ge[2], 64), ge[1], lane, 1)
-        c = f0[2, 0, rows, :]
-        gv = c * c * (1.0 / VERTICAL) * (p[0] - p[1]) * (a[0] - a[1])
+        a = tiles(vb, row, count)
+        right, left = to_right(a, lane, 1), to_left(a, lane, 1)
+        rows = pl.ds(row - TOP[0], count)
         for t in range(2):
-            c = f0[1, t, rows, :]
-            gs = c * c * (p[t] - pv[t, after, :]) * (a[t] - vb[t, after, :])
-            c = f0[1, t, before, :]
-            gn = c * c * (p[t] - pv[t, before, :]) * (a[t] - vb[t, before, :])
-            total_faces = ((ge[t] + gw[t]) + (gs + gn)) + gv
-            terms[me, t, pl.ds(row - TOP[0], count), :] = -0.5 * total_faces / perm[t, rows, :]
+            near = q[0, t, rows, :] * (a[t] - vb[t, before, :]) + q[1, t, rows, :] * (a[t] - vb[t, after, :])
+            side = q[2, t, rows, :] * (a[t] - right[t]) + q[3, t, rows, :] * (a[t] - left[t])
+            terms[me, t, rows, :] = (near + side) + q[4, t, rows, :] * (a[t] - a[t ^ 1])
 
     copies3 = []
     for half in range(2):
@@ -428,7 +440,7 @@
     for k in range(1, terms.shape[0]):
         value = value + terms[k]
     gradient_out[...] = value
-    for copy in copies1 + copies2 + copies3:
+    for copy in copies0 + copies1 + copies2 + copies3:
         copy.wait_send()
 
 
@@ -450,7 +462,7 @@
     def vmem(*shape):
         return pltpu.VMEM(shape, f32)
 
-    level = [(3, HEIGHT[k], LANES) for k in range(3)]
+    level = [(TILES, HEIGHT[k], LANES) for k in range(3)]
     dma = pltpu.SemaphoreType.DMA
     scratch = [
         pltpu.SMEM((FACIES,), f32), pltpu.SMEM((1, WELLS), jnp.int32), pltpu.SMEM((1, WELLS), f32),
@@ -463,8 +475,8 @@
         *[vmem(*level[0]) for _ in range(3)],
         *[vmem(*level[1]) for _ in range(3)],
         *[vmem(*level[2]) for _ in range(2)],
-        vmem(*level[0]), vmem(ns, *block),
-        dma((8,)), dma((8,)), dma((8,)), dma((8,)), dma((8,)), dma((2, ns - 1)), dma((2, ns - 1)),
+        vmem(*level[0]), vmem(5, *block), vmem(ns, *block),
+        *[dma((8,)) for _ in range(7)], dma((2, ns - 1)), dma((2, ns - 1)),
     ]
     shapes = ((1, *block), (1, *block), block)
     results = pl.pallas_call(

time: 35.2 us -> 31.6 us (0.90)
  Pallas kernels: 34.4 us -> 30.8 us
    pallas_call x1, Pallas kernels: 33.7 us -> 30.1 us  [shards(): pl.pallas_call(kernel, out_shape=tuple((vmem(*shape) for shape in shapes)...]
where the time goes in v3:
time: 31.6 us; the launch traced here: 31.5 us
  Pallas kernels  30.8 us (97%)
  between operations  0.64 us (2%)
    pallas_call x1, Pallas kernels, shards(): pl.pallas_call(kernel, out_shape=tuple((vmem(*shape) for shape in shapes)...  30.1 us
    pallas_call x1, Pallas kernels, shards(): pl.pallas_call(store, out_shape=tuple((jax.ShapeDtypeStruct(shape, f32) f...  0.7 us

profile of v3, /device:TPU:1, one launch (start us, length us, event | category | flops | bytes accessed | tf_op | source)
XLA Modules:
  0.0 31.5 jit_solution(4499631026427984870)
XLA Ops:
  0.6 30.1 %shard_map.103 = (f32[1,2,64,128]{3,2,1,0:T(8,128)S(1)}, f32[1,2,64,128]{3,2,1,0:T(8,128)S(1)}, f32[2,64,128]{2,1,0:T(8,128)S(1)}) custom-call(f32[2,64,128]{2,1,0:T(8,128)} %perm_log.1, s32[2,64,128]{2,1,0:T(8,128)} %facies.1, f32[4]{0:T(128)} %scale_in.1, f32[2,64,128]{2,1,0:T(8,128)} %accumulation.1, f32[1,2,64,128]{3,2,1,0:T(8,128)} %previous.1, ...), custom_call_target="tpu_custom_call" | custom-call | tf_op jit(solution)/shard_map/pallas_call | solution.py:482
  30.8 0.7 %shard_map.104 = (f32[1,2,64,128]{3,2,1,0:T(8,128)}, f32[1,2,64,128]{3,2,1,0:T(8,128)}, f32[2,64,128]{2,1,0:T(8,128)}) custom-call(f32[1,2,64,128]{3,2,1,0:T(8,128)S(1)} %get-tuple-element.6.refs_0_, f32[1,2,64,128]{3,2,1,0:T(8,128)S(1)} %get-tuple-element.7.refs_1_, f32[2,64,128]{2,1,0:T(8,128)S(1)} %get-tuple-element.8.refs_2_), custom_call_target="tpu_custom_call" | custom-call | tf_op jit(solution)/shard_map/pallas_call | solution.py:492

commit v4 on v3

--- a/solution.py
+++ b/solution.py
@@ -264,11 +264,31 @@
         pltpu.make_async_copy(rates_in, well_rates, load_sem.at[6]),
         pltpu.make_async_copy(observed.at[0], observed_v, load_sem.at[7]),
     ]
+    always, westward, eastward = (0, 1), (4, 6, 2), (5, 7, 3)
+    barrier = pltpu.get_barrier_semaphore()
+
+    def greet(targets):
+        for target in targets:
+            pl.semaphore_signal(barrier, inc=1, device_id=target, device_id_type=MESH)
+
+    def sideways(to_west, to_east):
+        pl.when(gy > 0)(to_west)
+        pl.when(gy < ny - 1)(to_east)
+
+    sideways(lambda: greet([around[k] for k in westward]), lambda: greet([around[k] for k in eastward]))
+    greet([around[k] for k in always] + peers)
     for copy in loads:
         copy.start()
-    barrier = pltpu.get_barrier_semaphore()
-    for target in around + peers:
-        pl.semaphore_signal(barrier, inc=1, device_id=target, device_id_type=MESH)
+
+    @pl.when(gy == 0)
+    def _():
+        from_west[...] = jnp.ones_like(from_west)
+        from_west2[...] = jnp.ones_like(from_west2)
+
+    @pl.when(gy == ny - 1)
+    def _():
+        from_east[...] = jnp.ones_like(from_east)
+        from_east2[...] = jnp.ones_like(from_east2)
 
     for copy in loads[:7]:
         copy.wait()
@@ -282,7 +302,8 @@
         for half in range(2):
             rows = pl.ds(TOP[0] + 32 * half, 32)
             pack(ext[field, 0, rows, :], ext[field, 1, rows, :], to_west, to_east, (field, pl.ds(16 * half, 16), slice(None)))
-    pl.semaphore_wait(barrier, len(around) + len(peers))
+    no_west, no_east = lax.div(ny - gy, ny), lax.div(gy + 1, ny)
+    pl.semaphore_wait(barrier, len(around) + len(peers) - 3 * (no_west + no_east))
 
     def exchange(block, w_out, e_out, w_in, e_in, send, recv):
         upper, lower = pl.ds(TOP[0], HALO), pl.ds(TOP[0] + ROWS - HALO, HALO)
@@ -306,9 +327,21 @@
             )
             for k, (source, target) in enumerate(pairs)
         ]
-        for k in (4, 5, 6, 7, 2, 3, 0, 1):
+        sideways(
+            lambda: [copies[k].start() for k in westward] and None,
+            lambda: [copies[k].start() for k in eastward] and None,
+        )
+        for k in always:
             copies[k].start()
         return copies
+
+    def wait_recv(copies):
+        for k in always:
+            copies[k].wait_recv()
+        sideways(
+            lambda: [copies[k].wait_recv() for k in eastward] and None,
+            lambda: [copies[k].wait_recv() for k in westward] and None,
+        )
 
     first, rest = pl.ds(0, 1), pl.ds(1, 2)
     copies0, copies1 = [
@@ -331,8 +364,7 @@
     over(0, -32, 96, sources)
 
     def receive(copies, fields):
-        for copy in copies:
-            copy.wait_recv()
+        wait_recv(copies)
         for field in fields:
             for block in range(4):
                 unpack(from_west, from_east, ext.at[field], (field, pl.ds(16 * block, 16), slice(None)), GUARD + 32 * block)
@@ -396,8 +428,7 @@
                 q[k, t, pl.ds(row - TOP[0], count), :] = factor * weight * (face * face) * (p[t] - value)
 
     over(0, 0, ROWS, gradient_weights)
-    for copy in copies2:
-        copy.wait_recv()
+    wait_recv(copies2)
     for block in range(4):
         unpack(from_west2, from_east2, ext2, (pl.ds(16 * block, 16), slice(None)), GUARD + 32 * block)
 
@@ -423,25 +454,33 @@
             side = q[2, t, rows, :] * (a[t] - right[t]) + q[3, t, rows, :] * (a[t] - left[t])
             terms[me, t, rows, :] = (near + side) + q[4, t, rows, :] * (a[t] - a[t ^ 1])
 
-    copies3 = []
-    for half in range(2):
-        over(0, 32 * half, 32 * half + 32, gradient)
-        part = terms.at[me, :, pl.ds(32 * half, 32), :]
-        for k, target in enumerate(peers):
-            copy = pltpu.make_async_remote_copy(
-                src_ref=part, dst_ref=part, send_sem=send3.at[half, k], recv_sem=recv3.at[half, k],
-                device_id=target, device_id_type=MESH,
-            )
-            copy.start()
-            copies3.append(copy)
+    over(0, 0, ROWS, gradient)
+    part = terms.at[me]
+    copies3 = [
+        pltpu.make_async_remote_copy(
+            src_ref=part, dst_ref=part, send_sem=send3.at[k], recv_sem=recv3.at[k],
+            device_id=target, device_id_type=MESH,
+        )
+        for k, target in enumerate(peers)
+    ]
+    for copy in copies3:
+        copy.start()
     for copy in copies3:
         copy.wait_recv()
     value = terms[0]
     for k in range(1, terms.shape[0]):
         value = value + terms[k]
     gradient_out[...] = value
-    for copy in copies0 + copies1 + copies2 + copies3:
+    for copy in copies3:
         copy.wait_send()
+    sent = (copies0, copies1, copies2)
+    for copies in sent:
+        for k in always:
+            copies[k].wait_send()
+    sideways(
+        lambda: [copies[k].wait_send() for copies in sent for k in westward] and None,
+        lambda: [copies[k].wait_send() for copies in sent for k in eastward] and None,
+    )
 
 
 def store(*refs):
@@ -476,7 +515,7 @@
         *[vmem(*level[1]) for _ in range(3)],
         *[vmem(*level[2]) for _ in range(2)],
         vmem(*level[0]), vmem(5, *block), vmem(ns, *block),
-        *[dma((8,)) for _ in range(7)], dma((2, ns - 1)), dma((2, ns - 1)),
+        *[dma((8,)) for _ in range(7)], dma((ns - 1,)), dma((ns - 1,)),
     ]
     shapes = ((1, *block), (1, *block), block)
     results = pl.pallas_call(

time: 31.6 us -> 26.2 us (0.83)
  the two profiles are of different devices: /device:TPU:1 before, /device:TPU:160 now
where the time goes in v4:
time: 26.2 us; the launch traced here: 26 us
  Pallas kernels  25.4 us (97%)
  between operations  0.64 us (2%)
    pallas_call x1, Pallas kernels, shards(): pl.pallas_call(kernel, out_shape=tuple((vmem(*shape) for shape in shapes)...  24.7 us
    pallas_call x1, Pallas kernels, shards(): pl.pallas_call(store, out_shape=tuple((jax.ShapeDtypeStruct(shape, f32) f...  0.7 us

profile of v4, /device:TPU:160, one launch (start us, length us, event | category | flops | bytes accessed | tf_op | source)
XLA Modules:
  0.0 26.0 jit_solution(15549900663307994566)
XLA Ops:
  0.6 24.7 %shard_map.103 = (f32[1,2,64,128]{3,2,1,0:T(8,128)S(1)}, f32[1,2,64,128]{3,2,1,0:T(8,128)S(1)}, f32[2,64,128]{2,1,0:T(8,128)S(1)}) custom-call(f32[2,64,128]{2,1,0:T(8,128)} %perm_log.1, s32[2,64,128]{2,1,0:T(8,128)} %facies.1, f32[4]{0:T(128)} %scale_in.1, f32[2,64,128]{2,1,0:T(8,128)} %accumulation.1, f32[1,2,64,128]{3,2,1,0:T(8,128)} %previous.1, ...), custom_call_target="tpu_custom_call" | custom-call | tf_op jit(solution)/shard_map/pallas_call | solution.py:521
  25.3 0.7 %shard_map.104 = (f32[1,2,64,128]{3,2,1,0:T(8,128)}, f32[1,2,64,128]{3,2,1,0:T(8,128)}, f32[2,64,128]{2,1,0:T(8,128)}) custom-call(f32[1,2,64,128]{3,2,1,0:T(8,128)S(1)} %get-tuple-element.6.refs_0_, f32[1,2,64,128]{3,2,1,0:T(8,128)S(1)} %get-tuple-element.7.refs_1_, f32[2,64,128]{2,1,0:T(8,128)S(1)} %get-tuple-element.8.refs_2_), custom_call_target="tpu_custom_call" | custom-call | tf_op jit(solution)/shard_map/pallas_call | solution.py:531

commit v5 on v4

--- a/solution.py
+++ b/solution.py
@@ -140,7 +140,7 @@
     over(level, low, high, body)
 
 
-def scale(faces, e, level, low, high):
+def gather(faces, e, level, low, high):
     s = 2**level
 
     def body(row, count):
@@ -149,16 +149,24 @@
         east = tiles(faces.at[0], row, count)
         west = to_left(east, lane, s)
         for t in range(TILES):
-            south = faces[1, t, rows, :]
-            north = faces[1, t, pl.ds(row - 1, count), :]
-            across = faces[2, t, rows, :]
-            diag = ((north + south) + (east[t] + west[t])) + (across + faces[3, t, rows, :])
+            ends = faces[1, t, pl.ds(row - 1, count), :] + faces[1, t, rows, :]
+            e[3, t, rows, :] = west[t]
+            e[6, t, rows, :] = (ends + (east[t] + west[t])) + faces[2, t, rows, :]
+
+    over(level, low, high, body)
+
+
+def scale(faces, e, level, low, high):
+    def body(row, count):
+        rows = pl.ds(row, count)
+        for t in range(TILES):
+            diag = e[6, t, rows, :] + faces[3, t, rows, :]
             w = DAMPING / diag
-            e[0, t, rows, :] = w * north
-            e[1, t, rows, :] = w * south
-            e[2, t, rows, :] = w * east[t]
-            e[3, t, rows, :] = w * west[t]
-            e[4, t, rows, :] = w * across
+            e[0, t, rows, :] = w * faces[1, t, pl.ds(row - 1, count), :]
+            e[1, t, rows, :] = w * faces[1, t, rows, :]
+            e[2, t, rows, :] = w * faces[0, t, rows, :]
+            e[3, t, rows, :] = w * e[3, t, rows, :]
+            e[4, t, rows, :] = w * faces[2, t, rows, :]
             e[5, t, rows, :] = w
             e[6, t, rows, :] = diag * (1.0 / DAMPING)
 
@@ -374,6 +382,9 @@
     fine_faces(perm, f0, gx, gy, nx, ny, -32, 96)
     coarsen(f0, f1, 1, -16, 48, (0, 1, 2))
     coarsen(f1, f2, 2, -8, 24, (0, 1, 2))
+    gather(f0, e0, 0, -32, 96)
+    gather(f1, e1, 1, -16, 48)
+    gather(f2, e2, 2, -8, 24)
     receive(copies1, (1, 2))
 
     def right_side(row, count):

time: 26.2 us -> 25.9 us (0.989)
  Pallas kernels: 25.4 us -> 25.1 us
    pallas_call x1, Pallas kernels: 24.7 us -> 24.4 us  [shards(): pl.pallas_call(kernel, out_shape=tuple((vmem(*shape) for shape in shapes)...]
where the time goes in v5:
time: 25.9 us; the launch traced here: 25.7 us
  Pallas kernels  25.1 us (97%)
  between operations  0.64 us (2%)
    pallas_call x1, Pallas kernels, shards(): pl.pallas_call(kernel, out_shape=tuple((vmem(*shape) for shape in shapes)...  24.4 us
    pallas_call x1, Pallas kernels, shards(): pl.pallas_call(store, out_shape=tuple((jax.ShapeDtypeStruct(shape, f32) f...  0.7 us

profile of v5, /device:TPU:160, one launch (start us, length us, event | category | flops | bytes accessed | tf_op | source)
XLA Modules:
  0.0 25.7 jit_solution(9098221688868396050)
XLA Ops:
  0.6 24.4 %shard_map.103 = (f32[1,2,64,128]{3,2,1,0:T(8,128)S(1)}, f32[1,2,64,128]{3,2,1,0:T(8,128)S(1)}, f32[2,64,128]{2,1,0:T(8,128)S(1)}) custom-call(f32[2,64,128]{2,1,0:T(8,128)} %perm_log.1, s32[2,64,128]{2,1,0:T(8,128)} %facies.1, f32[4]{0:T(128)} %scale_in.1, f32[2,64,128]{2,1,0:T(8,128)} %accumulation.1, f32[1,2,64,128]{3,2,1,0:T(8,128)} %previous.1, ...), custom_call_target="tpu_custom_call" | custom-call | tf_op jit(solution)/shard_map/pallas_call | solution.py:532
  25.0 0.7 %shard_map.104 = (f32[1,2,64,128]{3,2,1,0:T(8,128)}, f32[1,2,64,128]{3,2,1,0:T(8,128)}, f32[2,64,128]{2,1,0:T(8,128)}) custom-call(f32[1,2,64,128]{3,2,1,0:T(8,128)S(1)} %get-tuple-element.6.refs_0_, f32[1,2,64,128]{3,2,1,0:T(8,128)S(1)} %get-tuple-element.7.refs_1_, f32[2,64,128]{2,1,0:T(8,128)S(1)} %get-tuple-element.8.refs_2_), custom_call_target="tpu_custom_call" | custom-call | tf_op jit(solution)/shard_map/pallas_call | solution.py:542
